TPU v7x, 128 devices: a whole 4x4x4 slice. The times are simulated.
128 devices in a mesh: seq: 16 (over y_lo, x, core), fsdp: 8 (over y_hi, z).
Axes of the slice: x: 4, y: 4 (y_hi: 2, y_lo: 2; y = y_hi * 2 + y_lo), z: 4, core: 2. Of those that a mesh axis runs over, the one named last changes fastest.
Arguments:
- hidden: bfloat16 [8, 2048, 2560], P('fsdp', 'seq'), may hold values from -6 to 6
- queries: bfloat16 [8, 2048, 4096], P('fsdp', 'seq'), may hold values from -6 to 6
- doc_ids: int32 [8, 2048], P('fsdp'), may hold values from 0 to 7, never falling along the last dimension, each value on 1 to 1024 neighbouring positions
- kv_weight: bfloat16 [2560, 1024], P('fsdp'), may hold values from -0.125 to 0.125
- q_gain: float32 [128], replicated, may hold values from 0.5 to 1.5
- k_gain: float32 [128], replicated, may hold values from 0.5 to 1.5
- grad_out: bfloat16 [8, 2048, 4096], P('fsdp', 'seq'), may hold values from -6 to 6
Outputs:
- attended: bfloat16 [8, 2048, 4096], P('fsdp', 'seq')
- grad_queries: bfloat16 [8, 2048, 4096], P('fsdp', 'seq')
- grad_hidden: bfloat16 [8, 2048, 2560], P('fsdp', 'seq')
- grad_weight: bfloat16 [2560, 1024], P(('seq', 'fsdp'))
- grad_qgain: float32 [128], replicated
- grad_kgain: float32 [128], replicated
Inputs may be any that keep to these rules, and one draw needn't show every extreme that they name: `doc_ids`: rollout numbers never fall along a pack; each of the 8 rollouts has at least one token and one has exactly 1024.
All inputs are finite; a program needn't handle non-finite values.
Results may differ from a plain program's by a relative error of at most 0.017.
Values may be sent and summed in bfloat16 or wider, within the bound.
A program may use at most 128 MiB of HBM per device.

v0:
```python
import math

import jax
import jax.numpy as jnp
from jax import lax
from jax.sharding import PartitionSpec as P

epsilon = 1e-06


def normalize(values, gain):
    return values * lax.rsqrt(jnp.mean(values * values, axis=-1, keepdims=True) + epsilon) * gain


def shards(hidden, queries, doc_ids, kv_weight, q_gain, k_gain, grad_out):
    tokens = hidden[0]
    local_q = queries[0]
    local_grad = grad_out[0]
    docs = doc_ids[0]
    tok_dev = tokens.shape[0]
    pack = docs.shape[0]
    head_dim = q_gain.shape[0]
    kv_width = kv_weight.shape[1] // 2
    kv_heads = kv_width // head_dim
    q_heads = local_q.shape[1] // head_dim
    group = q_heads // kv_heads
    scale = 1.0 / math.sqrt(head_dim)
    first = lax.axis_index("seq") * tok_dev
    q_pos = first + jnp.arange(tok_dev, dtype=jnp.int32)
    q_docs = lax.dynamic_slice_in_dim(docs, first, tok_dev)
    projected = jnp.dot(
        tokens,
        lax.all_gather(kv_weight, "fsdp", axis=0, tiled=True),
        preferred_element_type=jnp.float32,
    )
    k_raw = projected[:, :kv_width].reshape(tok_dev, kv_heads, head_dim)
    keys = normalize(k_raw, k_gain).astype(jnp.bfloat16).reshape(tok_dev, kv_width)
    values = projected[:, kv_width:].astype(jnp.bfloat16)
    q_raw = local_q.astype(jnp.float32).reshape(tok_dev, q_heads, head_dim)
    q_normed = (
        normalize(q_raw, q_gain).astype(jnp.bfloat16).reshape(tok_dev, kv_heads, group, head_dim)
    )

    def block_mask(kstart, width):
        k_pos = kstart + jnp.arange(width, dtype=jnp.int32)
        k_docs = lax.dynamic_slice_in_dim(docs, kstart, width)
        return (q_docs[:, None] == k_docs[None, :]) & (k_pos[None, :] <= q_pos[:, None])

    def block_exp(key_block, mask):
        key_heads = key_block.reshape(-1, kv_heads, head_dim)
        scores = (
            jnp.einsum("qgjd,kgd->gjqk", q_normed, key_heads, preferred_element_type=jnp.float32)
            * scale
        )
        return jnp.where(mask[None, None], jnp.exp(scores), 0.0)

    def forward_block(carry, key_block, value_block, kstart):
        mask = block_mask(kstart, key_block.shape[0])

        def forward_live_block(state):
            expd = block_exp(key_block, mask)
            value_heads = value_block.reshape(-1, kv_heads, head_dim)
            numer = state[0] + jnp.einsum(
                "gjqk,kgd->qgjd",
                expd.astype(jnp.bfloat16),
                value_heads,
                preferred_element_type=jnp.float32,
            )
            return (numer, state[1] + jnp.sum(expd, axis=-1))

        def forward_dead_block(state):
            return state

        return lax.cond(jnp.any(mask), forward_live_block, forward_dead_block, carry)

    initial = (
        jnp.zeros((tok_dev, kv_heads, group, head_dim), jnp.float32),
        jnp.zeros((kv_heads, group, tok_dev), jnp.float32),
    )
    key_piece = lax.all_gather(keys, "seq", axis=0, tiled=True)
    value_piece = lax.all_gather(values, "seq", axis=0, tiled=True)
    rows = key_piece.shape[0]
    forward_width = math.gcd(rows, 512)

    def step(index, state):
        offset = index * forward_width
        key_block = lax.dynamic_slice_in_dim(key_piece, offset, forward_width)
        value_block = lax.dynamic_slice_in_dim(value_piece, offset, forward_width)
        return forward_block(state, key_block, value_block, offset)

    numer, total = lax.fori_loop(0, rows // forward_width, step, initial)
    all_keys, all_values = (
        lax.all_gather(keys, "seq", axis=0, tiled=True),
        lax.all_gather(values, "seq", axis=0, tiled=True),
    )
    attended = (numer / jnp.transpose(total, (2, 0, 1))[..., None]).astype(jnp.bfloat16)
    d_out = local_grad.reshape(tok_dev, kv_heads, group, head_dim)
    delta = jnp.sum(d_out.astype(jnp.float32) * attended.astype(jnp.float32), axis=-1)
    delta_heads = jnp.transpose(delta, (1, 2, 0))
    width = math.gcd(pack, 512)

    def backward_block(dq_sum, index):
        kstart = index * width
        key_block = lax.dynamic_slice_in_dim(all_keys, kstart, width)
        value_block = lax.dynamic_slice_in_dim(all_values, kstart, width)
        mask = block_mask(kstart, width)

        def backward_live_block(running):
            key_heads = key_block.reshape(width, kv_heads, head_dim)
            value_heads = value_block.reshape(width, kv_heads, head_dim)
            probs = block_exp(key_block, mask) / total[..., None]
            grad_values = jnp.einsum(
                "gjqk,qgjd->kgd",
                probs.astype(jnp.bfloat16),
                d_out,
                preferred_element_type=jnp.float32,
            )
            grad_probs = jnp.einsum(
                "qgjd,kgd->gjqk", d_out, value_heads, preferred_element_type=jnp.float32
            )
            grad_scores = (probs * (grad_probs - delta_heads[..., None])).astype(jnp.bfloat16)
            updated = (
                running
                + jnp.einsum(
                    "gjqk,kgd->qgjd", grad_scores, key_heads, preferred_element_type=jnp.float32
                )
                * scale
            )
            grad_keys = (
                jnp.einsum(
                    "gjqk,qgjd->kgd", grad_scores, q_normed, preferred_element_type=jnp.float32
                )
                * scale
            )
            both = jnp.concatenate(
                [grad_keys.reshape(width, kv_width), grad_values.reshape(width, kv_width)], axis=1
            )
            return (updated, both)

        def backward_dead_block(running):
            return (running, jnp.zeros((width, 2 * kv_width), jnp.float32))

        return lax.cond(jnp.any(mask), backward_live_block, backward_dead_block, dq_sum)

    grad_qn, key_terms = lax.scan(
        backward_block,
        jnp.zeros((tok_dev, kv_heads, group, head_dim), jnp.float32),
        jnp.arange(pack // width, dtype=jnp.int32),
    )
    key_grads = lax.psum_scatter(
        key_terms.reshape(pack, 2 * kv_width).astype(jnp.bfloat16),
        "seq",
        scatter_dimension=0,
        tiled=True,
    ).astype(jnp.float32)
    k_value, k_pull = jax.vjp(normalize, k_raw, k_gain)
    grad_kraw, local_kgain = k_pull(key_grads[:, :kv_width].reshape(tok_dev, kv_heads, head_dim))
    q_value, q_pull = jax.vjp(normalize, q_raw, q_gain)
    grad_qraw, local_qgain = q_pull(grad_qn.reshape(tok_dev, q_heads, head_dim))
    grad_qgain, grad_kgain = lax.psum((local_qgain, local_kgain), ("seq", "fsdp"))
    grad_queries = grad_qraw.reshape(tok_dev, q_heads * head_dim).astype(jnp.bfloat16)
    grad_kv = jnp.concatenate(
        [grad_kraw.reshape(tok_dev, kv_width), key_grads[:, kv_width:]], axis=1
    ).astype(jnp.bfloat16)
    grad_hidden = jnp.einsum(
        "tk,rk->tr",
        grad_kv,
        lax.all_gather(kv_weight, "fsdp", axis=0, tiled=True),
        preferred_element_type=jnp.float32,
    )
    weight_terms = jnp.einsum("tr,tk->rk", tokens, grad_kv, preferred_element_type=jnp.float32)
    grad_weight = lax.psum_scatter(weight_terms, ("seq", "fsdp"), scatter_dimension=0, tiled=True)
    attended_out = attended.reshape(tok_dev, q_heads * head_dim)
    return (
        attended_out[None],
        grad_queries[None],
        grad_hidden.astype(jnp.bfloat16)[None],
        grad_weight.astype(jnp.bfloat16),
        grad_qgain,
        grad_kgain,
    )


def solution(mesh):
    return jax.shard_map(
        shards,
        mesh=mesh,
        in_specs=(
            P("fsdp", "seq", None),
            P("fsdp", "seq", None),
            P("fsdp", None),
            P("fsdp", None),
            P(),
            P(),
            P("fsdp", "seq", None),
        ),
        out_specs=(
            P("fsdp", "seq", None),
            P("fsdp", "seq", None),
            P("fsdp", "seq", None),
            P(("seq", "fsdp"), None),
            P(),
            P(),
        ),
        check_vma=False,
    )
```

profile of v0, /device:TPU:1, one launch (start us, length us, event | category | flops | bytes accessed | tf_op | source)
XLA Modules:
  0.0 468.0 jit_solution(3081529239441204536)
XLA Ops:
  7.2 0.7 all-gather.4.cloned.1.call-update
  8.0 0.7 broadcast_bitcast_fusion.1
  8.6 84.9 %all-gather.4.cloned.1.call-done = bf16[2560,1024]{1,0:T(8,128)(2,1)} async-done(((bf16[320,1024]{1,0:T(8,128)(2,1)}), bf16[2560,1024]{1,0:T(8,128)(2,1)}) %all-gather.4.cloned.1.call-update) | async-done | bytes 5242896 | tf_op jit(solution)/shard_map/all_gather | solution.py:33
  93.5 3.3 fusion.26
  97.6 0.7 copy-done.10
  98.3 0.7 multiply_convert_fusion.1
  99.1 0.7 slice.40
  100.1 1.8 copy.191
  101.9 2.3 multiply_reduce_fusion.2
  104.2 0.7 copy.151
  104.9 0.7 fusion.29
  105.6 2.4 multiply_convert_fusion
  108.1 1.3 copy.153
  109.4 22.3 %all-gather.6.cloned.1.call-done = bf16[2048,512]{1,0:T(8,128)(2,1)} async-done(((bf16[128,512]{1,0:T(8,128)(2,1)}), bf16[2048,512]{1,0:T(8,128)(2,1)}) %all-gather.6.cloned.1.call-update) | async-done | bytes 2097168 | tf_op jit(solution)/shard_map/all_gather | solution.py:80
  131.7 4.0 copy.147
  135.7 31.8 %all-gather.8.cloned.1.call-done = bf16[2048,512]{1,0:T(8,128)(2,1)} async-done(((bf16[128,512]{1,0:T(8,128)(2,1)}), bf16[2048,512]{1,0:T(8,128)(2,1)}) %all-gather.8.cloned.1.call-update) | async-done | bytes 2097168 | tf_op jit(solution)/shard_map/all_gather | solution.py:81
  167.5 4.0 copy.148
  171.5 1.6 broadcast.161.clone
  173.0 14.9 %while.32 = (s32[]{:T(128)}, f32[128,4,8,128]{3,0,2,1:T(8,128)}, f32[4,8,128]{2,1,0:T(8,128)S(1)}, s32[128]{0:T(128)S(1)}, s32[2048]{0:T(1024)S(1)}, /*index=5*/...) while((s32[]{:T(128)}, f32[128,4,8,128]{3,0,2,1:T(8,128)}, ...), condition=%wide.region_7.8_spmd.clone, body=%wide.region_2.7_spmd.clone.sunk | while | flops 1087111808 | bytes 25440032 | solution.py:91
  173.1 0.9 fusion.52
  174.7 8.3 %conditional.6 = ((f32[128,4,8,128]{3,0,2,1:T(8,128)}, f32[4,8,128]{2,1,0:T(8,128)S(1)})) conditional(s32[]{:T(128)} %convert_element_type.132, (f32[128,4,8,128]{3,0,2,1:T(8,128)}, f32[4,8,128]{2,1,0:T(8,128)S(1)}) %tuple.110, (pred[128,512]{0,1:T(8,128)(4,1)S(1)}, bf16[2048,512]{0,1:T(8,128)(2,1)}, s32[]{:T(128)}, ...), branch_computations={%region_4.0_spmd, %region_5.6_spmd} | conditional | flops 1086849024 | bytes 25362460 | solution.py:74
  174.7 1.3 constant_dynamic-slice_fusion
  176.0 1.9 fusion.4
  177.9 5.0 %bitcast_add_fusion = f32[128,4,8,128]{3,0,2,1:T(8,128)} fusion(f32[128,4,8,128]{3,0,2,1:T(8,128)} %get-tuple-element.319, bf16[512,4,128,1]{0,2,3,1:T(8,128)(2,1)S(1)} %bitcast.135, f32[4,512,128,8]{2,1,3,0:T(8,128)S(1)} %get-tuple-element.644, pred[128,512]{0,1:T(8,128)(4,1)S(1)} %get-tuple-element.320), kind=kOutput, calls=%fused_computation.9 | convolution fusion | flops 543686656 | bytes 13172736 | tf_op jit(solution)/shard_map/while/body/eval_jaxpr/cond/branch_1_fun/gjqk,kgd->qgjd/dot_general | solution.py:63
  183.0 0.9 fusion.52
  184.7 0.9 fusion.52
  186.4 0.9 fusion.52
  187.9 2.9 copy.149
  190.8 3.0 multiply_reduce_fusion.1
  194.1 26.8 %while.33 = (s32[]{:T(128)}, f32[128,4,8,128]{3,0,2,1:T(8,128)S(1)}, bf16[4,512,1024]{1,2,0:T(8,128)(2,1)}, s32[128]{0:T(128)S(1)}, s32[4]{0:T(128)S(1)}, /*inde...) while((s32[]{:T(128)}, ...), condition=%wide.region_13.14_spmd.clone, body=%wide.region_9.13_spmd.clone.sunk | while | flops 2702967552 | bytes 63615356 | solution.py:145
  195.6 0.8 fusion.53
  197.1 10.8 %conditional.7 = (f32[128,4,8,128]{3,0,2,1:T(8,128)S(1)}, bf16[1,512,1024]{1,2,0:T(8,128)(2,1)S(1)}) conditional(s32[]{:T(128)} %convert_element_type.133, f32[128,4,8,128]{3,0,2,1:T(8,128)S(1)} %get-tuple-element.870, (pred[128,512]{0,1:T(8,128)(4,1)S(1)}, bf16[2048,512]{0,1:T(8,128)(2,1)}, s32[]{:T(128)}, bf16[128,4,8,128]{0,3,2,1:T(8,128)(2,1)}, ...), branch_computations={%region_11.11_spmd, %region_12.12_spmd} | conditional | flops 2702704640 | bytes 61440076 | solution.py:143
  197.2 1.8 constant_dynamic-slice_fusion.2
  199.0 2.0 fusion.17
  201.0 1.3 fusion.16
  202.4 1.5 fusion.20
  203.9 1.5 fusion.18
  205.5 2.4 bitcast_add_fusion.1
  207.9 1.1 constant_dynamic-update-slice_fusion.2
  210.3 0.8 fusion.53
  211.9 1.1 constant_dynamic-update-slice_fusion.2
  214.3 0.8 fusion.53
  215.9 1.0 constant_dynamic-update-slice_fusion.2
  218.2 0.8 fusion.53
  219.8 1.1 constant_dynamic-update-slice_fusion.2
  220.9 6.3 %copy.160 = bf16[4,512,1024]{2,1,0:T(8,128)(2,1)} copy(bf16[4,512,1024]{1,2,0:T(8,128)(2,1)} %get-tuple-element.376) | data formatting | bytes 8388608 | tf_op jit(solution)/shard_map/convert_element_type | solution.py:151
  227.3 0.7 copy-done.19
  228.0 1.9 mul.258
  230.0 2.8 mul.259
  232.7 2.5 copy.155
  235.3 3.1 fusion.24
  238.6 1.9 broadcast_in_dim.89
  240.5 2.7 broadcast_in_dim.90
  243.3 2.7 reshape.206
  246.0 2.3 copy.187
  248.3 2.6 multiply_reduce_fusion
  251.2 3.5 fusion.22
  254.7 72.6 %reduce-scatter.3.cloned.1.call-done = bf16[128,1024]{1,0:T(8,128)(2,1)} async-done(((bf16[2048,1024]{1,0:T(8,128)(2,1)}), bf16[128,1024]{1,0:T(8,128)(2,1)}) %reduce-scatter.3.cloned.1.call-update) | async-done | bytes 262160 | tf_op jit(solution)/shard_map/reduce_scatter | solution.py:150
  327.3 1.0 slice_convert_fusion.1
  329.2 5.6 %convolution_bitcast_fusion.1 = f32[2560,1024]{0,1:T(8,128)} fusion(bf16[1,128,2560]{2,1,0:T(8,128)(2,1)S(1)} %copy-done, bf16[128,512]{1,0:T(8,128)(2,1)S(1)} %get-tuple-element.652, bf16[128,512]{1,0:T(8,128)(2,1)S(1)} %get-tuple-element.650), kind=kOutput, calls=%fused_computation.34 | convolution fusion | flops 671612928 | bytes 11403264 | tf_op jit(solution)/shard_map/tr,tk->rk/dot_general | solution.py:171
  334.8 119.5 %all-reduce.3 = (bf16[2560,1024]{0,1:T(8,128)(2,1)}, f32[128]{0:T(128)}, f32[128]{0:T(128)}) all-reduce(f32[2560,1024]{0,1:T(8,128)} %convolution_bitcast_fusion.1, f32[128]{0:T(128)S(1)} %multiply_reduce_fusion, f32[128]{0:T(128)S(1)} %bitcast_reduce_fusion), channel_id=3, replica_groups=mesh['seq'=16,'fsdp'=8] {'seq','fsdp'}, use_global_device_ids=true, to_apply=%region_17.18.clone | all-reduce | flops 2621696 | bytes 15730688
  454.3 1.2 dynamic-slice_convert_fusion
  455.5 0.8 copy.163
  456.3 5.2 %fusion.21 = bf16[1,128,2560]{2,1,0:T(8,128)(2,1)} fusion(bf16[2560,1024]{1,0:T(8,128)(2,1)} %all-gather.4.cloned.1.call-done, bf16[128,512]{1,0:T(8,128)(2,1)S(1)} %get-tuple-element.652, bf16[128,512]{1,0:T(8,128)(2,1)S(1)} %get-tuple-element.650), kind=kOutput, calls=%fused_computation.36 | convolution fusion | flops 671940608 | bytes 6160384 | tf_op jit(solution)/shard_map/tk,rk->tr/dot_general | solution.py:165
  (127 shorter events, 6.5 us)
Async XLA Ops:
  7.2 86.3 %copy-start = (bf16[1,128,2560]{2,1,0:T(8,128)(2,1)S(1)}, bf16[1,128,2560]{2,1,0:T(8,128)(2,1)}, u32[]{:S(2)}) copy-start(bf16[1,128,2560]{2,1,0:T(8,128)(2,1)} %param.15) | copy-start | bytes 1966084
  7.2 86.3 %all-gather.4.cloned.1.call-start = ((), (), s32[]{:S(2)}) async-start(), calls=%async_computation.1 | async-start | bytes 5898240 | tf_op jit(solution)/shard_map/all_gather | solution.py:33
  7.9 123.8 %all-gather.6.cloned.1.call-start = ((), (), s32[]{:S(2)}) async-start(), calls=%async_computation.2 | async-start | bytes 2228224 | tf_op jit(solution)/shard_map/all_gather | solution.py:80
  8.6 89.0 %copy-start.21 = (f32[512]{0:T(512)}, f32[512]{0:T(512)S(1)}, u32[]{:S(2)}) copy-start(f32[512]{0:T(512)S(1)} %broadcast_bitcast_fusion.1) | copy-start | bytes 6148
  96.8 3.3 copy-start.6
  96.8 3.0 copy-start.5
  97.0 3.1 copy-start.8
  97.3 2.9 copy-start.23
  97.6 0.7 copy-start.10
  99.0 68.4 %all-gather.8.cloned.1.call-start = ((), (), s32[]{:S(2)}) async-start(), calls=%async_computation.3 | async-start | bytes 2228224 | tf_op jit(solution)/shard_map/all_gather | solution.py:81
  99.8 227.5 %reduce-scatter.3.cloned.1.call-start = ((), (), s32[]{:S(2)}) async-start(), calls=%async_computation.4 | async-start | bytes 4456448 | tf_op jit(solution)/shard_map/reduce_scatter | solution.py:150
  101.9 2.4 copy-start.12
  101.9 3.7 copy-start.25
  104.2 1.4 copy-start.17
  104.9 85.9 %copy-start.1 = (bf16[1,128,4096]{1,2,0:T(8,128)(2,1)}, bf16[1,128,4096]{1,2,0:T(8,128)(2,1)S(1)}, u32[]{:S(2)}) copy-start(bf16[1,128,4096]{1,2,0:T(8,128)(2,1)S(1)} %copy.151) | copy-start | bytes 3145732
  105.6 3.8 copy-start.15
  105.6 3.8 copy-start.20
  197.1 1.9 copy-start.13
  199.0 2.0 copy-start.2
  227.2 0.7 copy-start.19
  230.0 2.8 copy-start.26
  235.3 3.2 copy-start.18
  246.0 2.3 copy-start.16
  248.3 2.6 copy-start.3
  248.3 2.9 copy-start.4
  251.1 77.3 %copy-start.9 = (f32[128,4,128]{2,1,0:T(4,128)S(1)}, f32[128,4,128]{2,1,0:T(4,128)}, u32[]{:S(2)}) copy-start(f32[128,4,128]{2,1,0:T(4,128)} %copy-done.8) | copy-start | bytes 786436
  251.1 77.3 %copy-start.27 = (f32[128]{0:T(128)S(1)}, f32[128]{0:T(128)}, u32[]{:S(2)}) copy-start(f32[128]{0:T(128)} %param.20) | copy-start | bytes 1540
  251.2 77.6 %copy-start.24 = (f32[128,4]{0,1:T(4,128)S(1)}, f32[128,4]{0,1:T(4,128)}, u32[]{:S(2)}) copy-start(f32[128,4]{0,1:T(4,128)} %copy-done.23) | copy-start | bytes 6148
  254.7 74.4 %copy-start.7 = (f32[128,1024]{1,0:T(8,128)S(1)}, f32[128,1024]{1,0:T(8,128)}, u32[]{:S(2)}) copy-start(f32[128,1024]{1,0:T(8,128)} %copy-done.6) | copy-start | bytes 1572868
  254.7 74.4 %copy-start.11 = (f32[128,4,128]{2,1,0:T(4,128)S(1)}, f32[128,4,128]{2,1,0:T(4,128)}, u32[]{:S(2)}) copy-start(f32[128,4,128]{2,1,0:T(4,128)} %copy-done.10) | copy-start | bytes 786436
  254.7 74.4 %copy-start.22 = (f32[512]{0:T(512)S(1)}, f32[512]{0:T(512)}, u32[]{:S(2)}) copy-start(f32[512]{0:T(512)} %copy-done.21) | copy-start | bytes 6148
  327.3 1.8 copy-start.14
Sparse Core Ops, SparseCore 0:
  10.3 83.1 all-gather.3
  99.2 32.4 all-gather.5
  133.4 34.0 all-gather.7
  227.4 99.8 reduce-scatter.2
where the time goes:
time: 470 us; the launch traced here: 468 us
  waiting for transfers between devices  212 us (45%)
  blocking collectives  120 us (26%)
  local copies, waits for them, and re-layouts  56.5 us (12%)
  matrix products  29.8 us (6%)
  other arithmetic  27.3 us (6%)
  between operations  14.1 us (3%)
  loops' own time  8.37 us (2%)
    unnamed x1, blocking collectives  120 us
    all_gather x1, waiting for transfers between devices, shards(): lax.all_gather(kv_weight, 'fsdp', axis=0, tiled=True)  84.9 us
    reduce_scatter x1, waiting for transfers between devices, shards(): lax.psum_scatter(key_terms.reshape(pack, 2 * kv_width).astype(jnp.bfloat1...  72.6 us
    all_gather x1, waiting for transfers between devices, shards(): value_piece = lax.all_gather(values, 'seq', axis=0, tiled=True)  31.8 us
    all_gather x1, waiting for transfers between devices, shards(): key_piece = lax.all_gather(keys, 'seq', axis=0, tiled=True)  22.3 us
    unnamed x58, local copies, waits for them, and re-layouts  14.2 us
  transfers between devices with their start and end apart: 4, of which 4 were waited for; matrix products, arithmetic and copies ran while one was open for 9% of the time, Pallas kernels for 0%

commit v1 on v0

v1 whole, which is shorter than its diff:
```python
import math

import jax
import jax.numpy as jnp
from jax import lax
from jax.experimental import pallas as pl
from jax.experimental.pallas import tpu as pltpu
from jax.sharding import PartitionSpec as P

MESH = pl.DeviceIdType.MESH
BF = jnp.bfloat16
F32 = jnp.float32
EPS = 1e-06
TOK = 128
HD = 128
KVH = 4
GROUP = 8
D = 2560
ROWS = 320
WIN = 9
SCALE = 1.0 / math.sqrt(HD)
LOG2E = 1.4426950408889634
NT = (((1,), (1,)), ((), ()))


class Place:
    def __init__(self):
        s = lax.axis_index("seq")
        f = lax.axis_index("fsdp")
        self.s, self.f = s, f
        self.c = lax.rem(s, 2)
        self.x = lax.rem(lax.div(s, 2), 4)
        self.yl = lax.div(s, 8)
        self.yh = lax.div(f, 4)
        self.z = lax.rem(f, 4)
        self.k = lax.div(s, 2)

    def at(self, x=None, yl=None, yh=None, z=None, c=None):
        x = self.x if x is None else x
        yl = self.yl if yl is None else yl
        yh = self.yh if yh is None else yh
        z = self.z if z is None else z
        c = self.c if c is None else c
        return ((yl * 4 + x) * 2 + c, yh * 4 + z)

    def xs(self, d):
        return lax.rem(self.x + d, 4)

    def zs(self, d):
        return lax.rem(self.z + d, 4)


class Net:
    def __init__(self, send, recv):
        self.send, self.recv, self.n = send, recv, 0
        self.sent = []

    def copy(self, src, dst, dev):
        i = self.n
        self.n += 1
        return pltpu.make_async_remote_copy(
            src_ref=src,
            dst_ref=dst,
            send_sem=self.send.at[i],
            recv_sem=self.recv.at[i],
            device_id=dev,
            device_id_type=MESH,
        )

    def start(self, copy, cond=None):
        self.sent.append((copy, cond))
        when(cond, copy.start)

    def drain(self):
        for copy, cond in self.sent:
            when(cond, copy.wait_send)


def when(cond, fn):
    if cond is None:
        fn()
    else:
        pl.when(cond)(fn)


def greet(partners):
    barrier = pltpu.get_barrier_semaphore()
    for dev in partners:
        pl.semaphore_signal(barrier, inc=1, device_id=dev, device_id_type=MESH)
    pl.semaphore_wait(barrier, len(partners))


def piece_start(i, c, z):
    return ((i // 8) * 8 + ((i // 2) % 4) * 2 + c) * 160 + ((i % 2) * 4 + z) * 20


N1 = 64


def gather_kernel(
    hid, w, kg,
    wout, kwin, vwin, kraw, hout,
    wbuf, kbuf, vbuf, hT, hs, hpk, hrecv, acc, send, recv, loc,
):
    p = Place()
    net = Net(send, recv)
    c, x, z = p.c, p.x, p.z
    sib = p.at(c=1 - c)
    xp, xm = p.at(x=p.xs(1)), p.at(x=p.xs(3))
    zp, zm = p.at(z=p.zs(1)), p.at(z=p.zs(3))
    far = p.at(yh=1 - p.yh, yl=1 - p.yl)
    near = p.at(yl=1 - p.yl)
    zgroup = [p.at(z=p.zs(d), c=cc) for d in range(4) for cc in (c, 1 - c)][1:]

    loads = [
        pltpu.make_async_copy(w.at[:, pl.ds(j * 128, 128)], wbuf.at[p.f, j], loc.at[j])
        for j in range(8)
    ]
    for l in loads:
        l.start()
    greet([xp, xm, far, near] + zgroup)
    for l in loads:
        l.wait()

    c4 = c * 4
    fo = (1 - p.yh) * 4
    others = [fo + z, fo + p.zs(3), fo + p.zs(1), fo + p.zs(2)]
    home = p.yh * 4
    f_m, f_p, f_2 = home + p.zs(3), home + p.zs(1), home + p.zs(2)

    y_cp = net.copy(wbuf.at[p.f, c4 + x], wbuf.at[p.f, c4 + x], far)
    net.start(y_cp)
    zp_own, zm_own = [None, None], [None, None]
    for q in (0, 1):
        r = pl.ds(c4 + 2 * q, 2)
        zp_own[q] = net.copy(wbuf.at[p.f, r], wbuf.at[p.f, r], zp)
        net.start(zp_own[q])
        r = pl.ds(c4 + 2 * (1 - q), 2)
        zm_own[1 - q] = net.copy(wbuf.at[p.f, r], wbuf.at[p.f, r], zm)
        net.start(zm_own[1 - q])

    for f in range(8):
        hs[f] = hid[:, f * ROWS:(f + 1) * ROWS]
    for b in range(D // 128):
        hT[pl.ds(b * 128, 128), :] = hid[:, b * 128:(b + 1) * 128].astype(F32).T

    xp_cp, xm_cp = [None] * 4, [None] * 4

    def to_x(i):
        ref = wbuf.at[others[i], c4 + x]
        xp_cp[i] = net.copy(ref, ref, xp)
        xm_cp[i] = net.copy(ref, ref, xm)
        net.start(xp_cp[i])
        net.start(xm_cp[i])

    y_cp.wait_recv()
    quarter = wbuf.at[others[0], c4 + x]
    zp_oth = net.copy(quarter, quarter, zp)
    zm_oth = net.copy(quarter, quarter, zm)
    net.start(zp_oth)
    net.start(zm_oth)
    to_x(0)
    zp_own[0].wait_recv()
    r = pl.ds(c4, 2)
    zp_fwd = net.copy(wbuf.at[f_m, r], wbuf.at[f_m, r], zp)
    net.start(zp_fwd)
    zm_own[1].wait_recv()
    r = pl.ds(c4 + 2, 2)
    zm_fwd = net.copy(wbuf.at[f_p, r], wbuf.at[f_p, r], zm)
    net.start(zm_fwd)

    for zc in range(4):
        for cc in range(2):
            for i in range(16):
                hpk[zc * 2 + cc, pl.ds(i * 20, 20), :] = hT[pl.ds(piece_start(i, cc, zc), 20), :].astype(BF)

    zp_oth.wait_recv()
    ref = wbuf.at[others[1], c4 + x]
    zp_ofwd = net.copy(ref, ref, zp)
    net.start(zp_ofwd)
    to_x(1)
    zm_oth.wait_recv()
    to_x(2)
    zp_own[1].wait_recv()
    zm_own[0].wait_recv()

    def to_sib(f):
        r = pl.ds(c4, 4)
        cp = net.copy(wbuf.at[f, r], wbuf.at[f, r], sib)
        net.start(cp)
        return cp

    sib_cps = [(f_m, to_sib(f_m)), (f_p, to_sib(f_p))]
    zp_ofwd.wait_recv()
    to_x(3)
    x_fwd = []
    for i in range(4):
        if i < 2:
            xp_cp[i].wait_recv()
            ref = wbuf.at[others[i], c4 + p.xs(3)]
            cp = net.copy(ref, ref, xp)
        else:
            xm_cp[i].wait_recv()
            ref = wbuf.at[others[i], c4 + p.xs(1)]
            cp = net.copy(ref, ref, xm)
        net.start(cp)
        x_fwd.append(cp)
    zp_fwd.wait_recv()
    zm_fwd.wait_recv()
    sib_cps.append((f_2, to_sib(f_2)))

    mine = z * 2 + c
    h_cps = []
    for d in range(4):
        for e in range(2):
            if d == 0 and e == 0:
                continue
            zc = p.zs(d)
            cc = lax.rem(c + e, 2)
            cp = net.copy(hpk.at[zc * 2 + cc], hrecv.at[mine], p.at(z=zc, c=cc))
            net.start(cp)
            h_cps.append(cp)
    own_h = pltpu.make_async_copy(hpk.at[mine], hrecv.at[mine], loc.at[0])
    own_h.start()

    def shard(f):
        return jnp.concatenate([wbuf[f, j] for j in range(8)], axis=1)

    def project(f):
        return jnp.dot(hs[f], shard(f), preferred_element_type=F32)

    acc[...] = project(p.f)
    for f, cp in sib_cps:
        cp.wait_recv()
        acc[...] += project(f)
    rest = []
    for i in range(4):
        if i < 2:
            xm_cp[i].wait_recv()
        else:
            xp_cp[i].wait_recv()
        x_fwd[i].wait_recv()
        rest.append((others[i], to_sib(others[i])))
    for f, cp in rest:
        cp.wait_recv()
        acc[...] += project(f)
    w_save = pltpu.make_async_copy(wbuf, wout, loc.at[1])
    w_save.start()

    for d in range(1, WIN):
        @pl.when(p.s < d)
        def _():
            kbuf[d] = jnp.zeros((KVH, TOK, HD), BF)
            vbuf[d] = jnp.zeros((KVH, TOK, HD), BF)
    for g in range(KVH):
        raw = acc[:, g * HD:(g + 1) * HD]
        kraw[g] = raw
        r = lax.rsqrt(jnp.mean(raw * raw, axis=1, keepdims=True) + EPS)
        kbuf[0, g] = (raw * r * kg[...]).astype(BF)
        vbuf[0, g] = acc[:, 512 + g * HD:512 + (g + 1) * HD].astype(BF)

    row1 = p.yl == 1
    bufs = (kbuf, vbuf)
    y_c, r_c, l_c, r2_c, l2_c = [], [], [], [], []
    sc = [[None] * 5, [None] * 5]

    def sib_copy(ch, m):
        b = bufs[ch]
        cp = net.copy(b.at[2 * m], b.at[jnp.clip(2 * m + 1 - 2 * c, 0, WIN - 1)], sib)
        cond = p.k >= m
        if m == 4:
            cond = cond & (c == 1)
        if m == 0:
            cond = c == 0
        net.start(cp, cond)
        sc[ch][m] = cp

    for ch in range(2):
        b = bufs[ch]
        cp = net.copy(b.at[0], b.at[8], near)
        net.start(cp, p.yl == 0)
        y_c.append(cp)
        cp = net.copy(b.at[jnp.where(x < 3, 0, 8)], b.at[2], xp)
        net.start(cp, x < 3)
        r_c.append(cp)
        cp = net.copy(b.at[jnp.where(x == 0, 0, 8)], b.at[6], xm)
        net.start(cp, x == 0)
        l_c.append(cp)
        sib_copy(ch, 0)
    for ch in range(2):
        when(row1, y_c[ch].wait_recv)
        net.start(r_c[ch], (x == 3) & row1)
        net.start(l_c[ch], (x > 0) & row1)
    mid = (x == 1) | (x == 2)
    for ch in range(2):
        b = bufs[ch]
        when(p.k >= 1, r_c[ch].wait_recv)
        cp = net.copy(b.at[2], b.at[4], xp)
        net.start(cp, mid)
        r2_c.append(cp)
        sib_copy(ch, 1)
    for ch in range(2):
        b = bufs[ch]
        when(p.k >= 3, l_c[ch].wait_recv)
        cp = net.copy(b.at[6], b.at[4], xm)
        net.start(cp, mid & row1)
        l2_c.append(cp)
        sib_copy(ch, 3)
        sib_copy(ch, 4)
    for ch in range(2):
        when(x >= 2, r2_c[ch].wait_recv)
        when((x < 2) & row1, l2_c[ch].wait_recv)
        sib_copy(ch, 2)
    for ch in range(2):
        for m in range(5):
            cond = p.k >= m
            if m == 0:
                cond = c == 1
            if m == 4:
                cond = cond & (c == 0)
            when(cond, sc[ch][m].wait_recv)
    k_save = pltpu.make_async_copy(kbuf, kwin, loc.at[2])
    v_save = pltpu.make_async_copy(vbuf, vwin, loc.at[3])
    k_save.start()
    v_save.start()
    for cp in h_cps:
        cp.wait_recv()
    own_h.wait()
    h_save = pltpu.make_async_copy(hrecv, hout, loc.at[4])
    h_save.start()
    w_save.wait()
    k_save.wait()
    v_save.wait()
    h_save.wait()
    net.drain()
    assert net.n <= N1


def attend_kernel(
    sref, docs, q, do, kk, vv, qg,
    att, dq, dk, dv, qgain,
    mask, w_s, ds_s, qn_s, do_s, gacc,
):
    g = pl.program_id(0)
    s = sref[0]
    rows = WIN * TOK

    @pl.when(g == 0)
    def _():
        gacc[...] = jnp.zeros_like(gacc)
        qd = docs[pl.ds(s, 1), :].astype(F32)
        tri = (
            lax.broadcasted_iota(jnp.int32, (TOK, TOK), 0)
            <= lax.broadcasted_iota(jnp.int32, (TOK, TOK), 1)
        )
        for d in range(WIN):
            kd = docs[pl.ds(jnp.maximum(s - d, 0), 1), :].astype(F32)
            kd = jnp.broadcast_to(kd, (TOK, TOK)).T
            live = (kd == qd) & (s >= d)
            if d == 0:
                live = live & tri
            mask[pl.ds(d * TOK, TOK), :] = jnp.where(live, 1.0, 0.0).astype(F32)

    kall = kk[...].reshape(rows, HD)
    vall = vv[...].reshape(rows, HD)
    kT = kall.astype(F32).T.astype(BF)
    vT = vall.astype(F32).T.astype(BF)
    gain = jnp.broadcast_to(qg[...], (HD, HD)).T
    gain = jnp.concatenate([gain, gain], axis=1)
    for pair in range(GROUP // 2):
        cols = pl.ds(pair * 256, 256)
        heads = [2 * pair, 2 * pair + 1]

        def turned(ref):
            return jnp.concatenate(
                [ref[:, h * HD:(h + 1) * HD].astype(F32).T for h in heads], axis=1
            )

        qT = turned(q)
        doT = turned(do)
        r = lax.rsqrt(jnp.mean(qT * qT, axis=0, keepdims=True) + EPS)
        xhat = qT * r
        qn = (xhat * gain).astype(BF)
        qn_s[:, cols] = qn
        scores = jnp.dot(kall, qn, preferred_element_type=F32)
        m = mask[...]
        e = jnp.exp2(scores * (SCALE * LOG2E)) * jnp.concatenate([m, m], axis=1)
        total = jnp.sum(e, axis=0, keepdims=True)
        w = e.astype(BF)
        w_s[:, cols] = w
        inv = 1.0 / total
        attT = (jnp.dot(vT, w, preferred_element_type=F32) * inv).astype(BF).astype(F32)
        delta = jnp.sum(doT * attT, axis=0, keepdims=True) * inv
        dos = (doT * inv).astype(BF)
        do_s[:, cols] = dos
        dp = jnp.dot(vall, dos, preferred_element_type=F32)
        ds = (e * (dp - delta)).astype(BF)
        ds_s[:, cols] = ds
        dy = jnp.dot(kT, ds, preferred_element_type=F32) * SCALE
        gacc[...] += dy * xhat
        dxh = dy * gain
        dx = r * (dxh - xhat * jnp.mean(xhat * dxh, axis=0, keepdims=True))
        for n, h in enumerate(heads):
            att[:, h * HD:(h + 1) * HD] = attT[:, n * HD:(n + 1) * HD].T.astype(BF)
            dq[:, h * HD:(h + 1) * HD] = dx[:, n * HD:(n + 1) * HD].T.astype(BF)
    dvv = lax.dot_general(w_s[...], do_s[...], NT, preferred_element_type=F32)
    dv[...] = dvv.astype(BF).reshape(WIN, 1, TOK, HD)
    dkk = lax.dot_general(ds_s[...], qn_s[...], NT, preferred_element_type=F32) * SCALE
    dk[...] = dkk.astype(BF).reshape(WIN, 1, TOK, HD)

    @pl.when(g == KVH - 1)
    def _():
        a = gacc[:, :HD] + gacc[:, HD:]
        qgain[...] = jnp.sum(a.T, axis=0, keepdims=True)


N3 = 96


def reduce_kernel(
    dk, dv, kraw, wfull, hbuf, kg, qgain,
    gh, gw, qgo, kgo,
    pk, pv, sbk, sbv, r2r, r2l, r1, r3, ry, t0,
    wbuf, hb, gk, gv, gf, st, rbs, rbr, stf, gs1, gr1, gs2, gr2, send, recv, loc,
):
    p = Place()
    net = Net(send, recv)
    c, x, z, k = p.c, p.x, p.z, p.k
    row1 = p.yl == 1
    sib = p.at(c=1 - c)
    xp, xm = p.at(x=p.xs(1)), p.at(x=p.xs(3))
    zp, zm = p.at(z=p.zs(1)), p.at(z=p.zs(3))
    near = p.at(yl=1 - p.yl)
    zgroup = [p.at(z=p.zs(d), c=cc) for d in range(4) for cc in (c, 1 - c)][1:]
    me16 = (p.yl * 4 + x) * 2 + p.yh
    peers = []
    for i in range(1, 16):
        o = lax.rem(me16 + i, 16)
        peers.append((o, p.at(x=lax.rem(lax.div(o, 2), 4), yl=lax.div(o, 8), yh=lax.rem(o, 2))))

    parts = (pk, pv)
    sbs = (sbk, sbv)
    loads = [
        pltpu.make_async_copy(dv, pv, loc.at[1]),
        pltpu.make_async_copy(dk, pk, loc.at[0]),
        pltpu.make_async_copy(wfull, wbuf, loc.at[2]),
        pltpu.make_async_copy(hbuf, hb, loc.at[3]),
    ]
    for l in loads:
        l.start()
    greet(zgroup + [d for _, d in peers])
    loads[0].wait()
    loads[1].wait()

    order = (1, 0)
    sc = [[None] * 5, [None] * 5]
    for ch in order:
        for m in (2, 1, 3, 4, 0):
            cp = net.copy(parts[ch].at[jnp.clip(2 * m + 2 * c - 1, 0, WIN - 1)], sbs[ch].at[m], sib)
            cond = k >= m
            if m == 0:
                cond = c == 1
            if m == 4:
                cond = cond & (c == 0)
            net.start(cp, cond)
            sc[ch][m] = cp

    def pair(ch, m):
        cond = k >= m
        if m == 0:
            cond = c == 0
        if m == 4:
            cond = cond & (c == 1)

        def add():
            sc[ch][m].wait_recv()
            if m == 0:
                t0[ch] = t0[ch] + sbs[ch][m].astype(F32)
            else:
                b = parts[ch]
                b[2 * m] = (b[2 * m].astype(F32) + sbs[ch][m].astype(F32)).astype(BF)

        when(cond, add)

    def add_to(ch, slot, ref):
        def add():
            if slot == 0:
                t0[ch] = t0[ch] + ref[ch].astype(F32)
            else:
                b = parts[ch]
                b[slot] = (b[slot].astype(F32) + ref[ch].astype(F32)).astype(BF)
        return add

    def arrive(cond, cp, fn):
        def go():
            cp.wait_recv()
            fn()
        when(cond, go)

    mid = (x == 1) | (x == 2)
    c2r, c2l, c1, c3, cy = [None] * 2, [None] * 2, [None] * 2, [None] * 2, [None] * 2
    for ch in order:
        pair(ch, 2)
        b = parts[ch]
        c2r[ch] = net.copy(b.at[4], r2r.at[ch], xm)
        net.start(c2r[ch], x >= 2)
        c2l[ch] = net.copy(b.at[4], r2l.at[ch], xp)
        net.start(c2l[ch], (x < 2) & row1)
    for ch in order:
        pair(ch, 1)
        pair(ch, 3)
        pair(ch, 4)
    for ch in order:
        b = parts[ch]
        arrive(mid, c2r[ch], add_to(ch, 2, r2r))
        c1[ch] = net.copy(b.at[2], r1.at[ch], xm)
        net.start(c1[ch], k >= 1)
        arrive(mid & row1, c2l[ch], add_to(ch, 6, r2l))
        c3[ch] = net.copy(b.at[6], r3.at[ch], xp)
        net.start(c3[ch], k >= 3)
    for ch in order:
        t0[ch] = parts[ch][0].astype(F32)
        pair(ch, 0)
    for ch in order:
        arrive(x < 3, c1[ch], add_to(ch, 0, r1))
        arrive((x == 3) & row1, c1[ch], add_to(ch, 8, r1))
        arrive(x == 0, c3[ch], add_to(ch, 0, r3))
        arrive((x > 0) & row1, c3[ch], add_to(ch, 8, r3))
        cy[ch] = net.copy(parts[ch].at[8], ry.at[ch], near)
        net.start(cy[ch], row1)

    mine = z * 2 + c
    bufs = (gk, gv)
    zpc, zmc, sibc, fwd = [None] * 2, [None] * 2, [None] * 2, [None] * 2
    for ch in order:
        arrive(p.yl == 0, cy[ch], add_to(ch, 0, ry))
        if ch == 0:
            kga = jnp.zeros((1, HD), F32)
            for g in range(KVH):
                raw = kraw[g]
                r = lax.rsqrt(jnp.mean(raw * raw, axis=1, keepdims=True) + EPS)
                xh = raw * r
                dy = t0[0, g]
                kga = kga + jnp.sum(dy * xh, axis=0, keepdims=True)
                dxh = dy * kg[...]
                dx = r * (dxh - xh * jnp.mean(xh * dxh, axis=1, keepdims=True))
                gk[mine, g] = dx.astype(BF)
            gs1[...] = jnp.concatenate(
                [qgain[...], kga, jnp.zeros((6, HD), F32)], axis=0
            )
        else:
            gv[mine] = t0[1].astype(BF)
        b = bufs[ch]
        zpc[ch] = net.copy(b.at[mine], b.at[mine], zp)
        zmc[ch] = net.copy(b.at[mine], b.at[mine], zm)
        sibc[ch] = net.copy(b.at[mine], b.at[mine], sib)
        net.start(zpc[ch])
        net.start(zmc[ch])
        net.start(sibc[ch])
    g1 = []
    for d in range(4):
        for e in range(2):
            if d == 0 and e == 0:
                continue
            cp = net.copy(gs1, gr1.at[mine], p.at(z=p.zs(d), c=lax.rem(c + e, 2)))
            net.start(cp)
            g1.append(cp)

    def slot(d):
        return p.zs(d) * 2 + c

    def forward(ch, d, dev):
        cp = net.copy(bufs[ch].at[slot(d)], bufs[ch].at[slot(d)], dev)
        net.start(cp)
        return cp

    zmc[1].wait_recv()
    fwd[1] = forward(1, 1, zm)
    s_p1 = forward(1, 1, sib)
    zpc[1].wait_recv()
    s_m1 = forward(1, 3, sib)
    zpc[0].wait_recv()
    fwd[0] = forward(0, 3, zp)
    s_m0 = forward(0, 3, sib)
    zmc[0].wait_recv()
    s_p0 = forward(0, 1, sib)

    loads[2].wait()
    gkv = jnp.concatenate(
        [gk[mine, g] for g in range(KVH)] + [gv[mine, g] for g in range(KVH)], axis=1
    )
    for f in range(8):
        wv = jnp.concatenate([wbuf[f, j] for j in range(8)], axis=1)
        gh[:, f * ROWS:(f + 1) * ROWS] = lax.dot_general(
            gkv, wv, NT, preferred_element_type=F32
        ).astype(BF)

    fwd[1].wait_recv()
    s_f1 = forward(1, 2, sib)
    fwd[0].wait_recv()
    s_f0 = forward(0, 2, sib)
    for cp in g1:
        cp.wait_recv()
    gr1[mine] = gs1[...]
    gs2[...] = jnp.sum(gr1[...], axis=0)
    g2 = []
    for i, (o, dev) in enumerate(peers):
        cp = net.copy(gs2, gr2.at[me16], dev)
        net.start(cp)
        g2.append(cp)
    gr2[me16] = gs2[...]
    loads[3].wait()
    for cp in (sibc[1], s_p1, s_m1, s_f1, sibc[0], s_p0, s_m0, s_f0):
        cp.wait_recv()

    lhs = jnp.concatenate([hb[i] for i in range(8)], axis=1)
    for ch in order:
        for j in range(KVH):
            rhs = bufs[ch][:, j].reshape(8 * TOK, HD)
            gf[:, (ch * 4 + j) * HD:(ch * 4 + j + 1) * HD] = jnp.dot(lhs, rhs, preferred_element_type=F32)
    for i in range(16):
        for j in range(8):
            st[i, pl.ds(j * 20, 20), :] = gf[pl.ds(i * 20, 20), j * HD:(j + 1) * HD]
    for i in range(16):
        rbs[i] = st[i].astype(BF)
    w_c = []
    for i, (o, dev) in enumerate(peers):
        cp = net.copy(rbs.at[o], rbr.at[me16], dev)
        net.start(cp)
        w_c.append(cp)
    rbr[me16] = rbs[me16]
    for cp in w_c:
        cp.wait_recv()
    total = rbr[0].astype(F32)
    for i in range(1, 16):
        total = total + rbr[i].astype(F32)
    stf[...] = total
    for j in range(8):
        gw[:, j * HD:(j + 1) * HD] = stf[pl.ds(j * 20, 20), :].astype(BF)
    for cp in g2:
        cp.wait_recv()
    gsum = jnp.sum(gr2[...], axis=0)
    qgo[...] = gsum[0:1]
    kgo[...] = gsum[1:2]
    net.drain()
    assert net.n <= N3


def shards(hidden, queries, doc_ids, kv_weight, q_gain, k_gain, grad_out):
    hid = hidden[0]
    vm = pl.BlockSpec(memory_space=pltpu.VMEM)
    hbm = pl.BlockSpec(memory_space=pl.ANY)
    kg = k_gain.reshape(1, HD)
    qg = q_gain.reshape(1, HD)
    sds = jax.ShapeDtypeStruct
    win = (WIN, KVH, TOK, HD)
    wfull, kwin, vwin, kraw, hbuf = pl.pallas_call(
        gather_kernel,
        out_shape=(
            sds((8, 8, ROWS, 128), BF),
            sds(win, BF),
            sds(win, BF),
            sds((KVH, TOK, HD), F32),
            sds((8, ROWS, TOK), BF),
        ),
        in_specs=[vm, hbm, vm],
        out_specs=(hbm, hbm, hbm, vm, hbm),
        scratch_shapes=[
            pltpu.VMEM((8, 8, ROWS, 128), BF),
            pltpu.VMEM(win, BF),
            pltpu.VMEM(win, BF),
            pltpu.VMEM((D, TOK), F32),
            pltpu.VMEM((8, TOK, ROWS), BF),
            pltpu.VMEM((8, ROWS, TOK), BF),
            pltpu.VMEM((8, ROWS, TOK), BF),
            pltpu.VMEM((TOK, 1024), F32),
            pltpu.SemaphoreType.DMA((N1,)),
            pltpu.SemaphoreType.DMA((N1,)),
            pltpu.SemaphoreType.DMA((8,)),
        ],
        compiler_params=pltpu.CompilerParams(
            collective_id=0, has_side_effects=True, vmem_limit_bytes=56 * 1024 * 1024
        ),
        name="gather",
    )(hid, kv_weight, kg)

    s = lax.axis_index("seq").astype(jnp.int32).reshape(1)
    docs = doc_ids[0].reshape(16, TOK)
    rows = WIN * TOK
    head = pl.BlockSpec((TOK, GROUP * HD), lambda g: (0, g))
    wspec = pl.BlockSpec((WIN, 1, TOK, HD), lambda g: (0, g, 0, 0))
    fixed = pl.BlockSpec((1, HD), lambda g: (0, 0))
    att, dq, dk, dv, qgain = pl.pallas_call(
        attend_kernel,
        grid=(KVH,),
        out_shape=(
            sds((TOK, 32 * HD), BF),
            sds((TOK, 32 * HD), BF),
            sds(win, BF),
            sds(win, BF),
            sds((1, HD), F32),
        ),
        in_specs=[
            pl.BlockSpec(memory_space=pltpu.SMEM),
            pl.BlockSpec((16, TOK), lambda g: (0, 0)),
            head,
            head,
            wspec,
            wspec,
            fixed,
        ],
        out_specs=(head, head, wspec, wspec, fixed),
        scratch_shapes=[
            pltpu.VMEM((rows, TOK), F32),
            pltpu.VMEM((rows, GROUP * TOK), BF),
            pltpu.VMEM((rows, GROUP * TOK), BF),
            pltpu.VMEM((HD, GROUP * TOK), BF),
            pltpu.VMEM((HD, GROUP * TOK), BF),
            pltpu.VMEM((HD, 256), F32),
        ],
        compiler_params=pltpu.CompilerParams(vmem_limit_bytes=56 * 1024 * 1024),
        name="attend",
    )(s, docs, queries[0], grad_out[0], kwin, vwin, qg)

    unit = (KVH, TOK, HD)
    gh, gw, qgo, kgo = pl.pallas_call(
        reduce_kernel,
        out_shape=(
            sds((TOK, D), BF),
            sds((20, 1024), BF),
            sds((1, HD), F32),
            sds((1, HD), F32),
        ),
        in_specs=[hbm, hbm, vm, hbm, hbm, vm, vm],
        out_specs=(vm, vm, vm, vm),
        scratch_shapes=[
            pltpu.VMEM(win, BF),
            pltpu.VMEM(win, BF),
            pltpu.VMEM((5,) + unit, BF),
            pltpu.VMEM((5,) + unit, BF),
            pltpu.VMEM((2,) + unit, BF),
            pltpu.VMEM((2,) + unit, BF),
            pltpu.VMEM((2,) + unit, BF),
            pltpu.VMEM((2,) + unit, BF),
            pltpu.VMEM((2,) + unit, BF),
            pltpu.VMEM((2,) + unit, F32),
            pltpu.VMEM((8, 8, ROWS, 128), BF),
            pltpu.VMEM((8, ROWS, TOK), BF),
            pltpu.VMEM((8,) + unit, BF),
            pltpu.VMEM((8,) + unit, BF),
            pltpu.VMEM((ROWS, 1024), F32),
            pltpu.VMEM((16, 160, HD), F32),
            pltpu.VMEM((16, 160, HD), BF),
            pltpu.VMEM((16, 160, HD), BF),
            pltpu.VMEM((160, HD), F32),
            pltpu.VMEM((8, HD), F32),
            pltpu.VMEM((8, 8, HD), F32),
            pltpu.VMEM((8, HD), F32),
            pltpu.VMEM((16, 8, HD), F32),
            pltpu.SemaphoreType.DMA((N3,)),
            pltpu.SemaphoreType.DMA((N3,)),
            pltpu.SemaphoreType.DMA((4,)),
        ],
        compiler_params=pltpu.CompilerParams(
            collective_id=1, has_side_effects=True, vmem_limit_bytes=56 * 1024 * 1024
        ),
        name="reduce",
    )(dk, dv, kraw, wfull, hbuf, kg, qgain)
    return (att[None], dq[None], gh[None], gw, qgo.reshape(HD), kgo.reshape(HD))


def solution(mesh):
    return jax.shard_map(
        shards,
        mesh=mesh,
        in_specs=(
            P("fsdp", "seq", None),
            P("fsdp", "seq", None),
            P("fsdp", None),
            P("fsdp", None),
            P(),
            P(),
            P("fsdp", "seq", None),
        ),
        out_specs=(
            P("fsdp", "seq", None),
            P("fsdp", "seq", None),
            P("fsdp", "seq", None),
            P(("seq", "fsdp"), None),
            P(),
            P(),
        ),
        check_vma=False,
    )
```

time: 470 us -> 133 us (0.28)
  waiting for transfers between devices: 212 us -> 0 us
  Pallas kernels: 0 us -> 128 us
  blocking collectives: 120 us -> 0 us
  local copies, waits for them, and re-layouts: 56.5 us -> 3.62 us
  matrix products: 29.8 us -> 0 us
  other arithmetic: 27.3 us -> 0 us
  between operations: 14.1 us -> 0.68 us
  loops' own time: 8.37 us -> 0 us
    all_gather x3 -> x0, waiting for transfers between devices: 139 us -> none  [the longest x1 84.9 us: shards(): lax.all_gather(kv_weight, 'fsdp', axis=0, tiled=True)]
    pallas_call x0 -> x3, Pallas kernels: none -> 128 us  [the longest x1 62.8 us: shards(): pl.pallas_call(reduce_kernel, out_shape=(sds((TOK, D), BF), sds((20, 1024...]
    unnamed x1 -> x0, blocking collectives: 120 us -> none
    reduce_scatter x1 -> x0, waiting for transfers between devices: 72.6 us -> none  [shards(): lax.psum_scatter(key_terms.reshape(pack, 2 * kv_width).astype(jnp.bfloat1...]
    dot_general x10 -> x0, matrix products: 29.8 us -> none  [the longest x1 5.55 us: shards(): jnp.einsum('tr,tk->rk', tokens, grad_kv, preferred_element_type=jnp.float32)]
    reduce_sum x8 -> x0, other arithmetic: 11.6 us -> none  [the longest x5 6.06 us: normalize(): values * lax.rsqrt(jnp.mean(values * values, axis=-1, keepdims=True) + ep...]
    unnamed x58 -> x10, local copies, waits for them, and re-layouts: 14.2 us -> 3.62 us
    another operation x10 -> x0, loops' own time: 8.37 us -> none  [the longest x1 5.47 us: shards(): lax.scan(backward_block, jnp.zeros((tok_dev, kv_heads, group, head_dim),...]
  transfers between devices with their start and end apart: 4 -> 0, of which waited for: 4 -> 0; matrix products, arithmetic and copies ran while one was open for 9% -> 0% of each run, Pallas kernels for 0% -> 0%
where the time goes in v1:
time: 133 us
  Pallas kernels  128 us (96%)
  local copies, waits for them, and re-layouts  3.62 us (3%)
    pallas_call x1, Pallas kernels, shards(): pl.pallas_call(reduce_kernel, out_shape=(sds((TOK, D), BF), sds((20, 1024...  62.8 us
    pallas_call x1, Pallas kernels, shards(): pl.pallas_call(gather_kernel, out_shape=(sds((8, 8, ROWS, 128), BF), sds(...  41.6 us
    pallas_call x1, Pallas kernels, shards(): pl.pallas_call(attend_kernel, grid=(KVH,), out_shape=(sds((TOK, 32 * HD),...  24 us
    unnamed x10, local copies, waits for them, and re-layouts  3.62 us

profile of v1, /device:TPU:1, one launch (start us, length us, event | category | flops | bytes accessed | tf_op | source)
XLA Modules:
  0.0 132.7 jit_solution(4368164521009306993)
XLA Ops:
  0.6 41.6 %gather.1 = (bf16[8,8,320,128]{3,2,1,0:T(8,128)(2,1)}, bf16[9,4,128,128]{3,2,1,0:T(8,128)(2,1)}, bf16[9,4,128,128]{3,2,1,0:T(8,128)(2,1)}, f32[4,128,128]{2,1,0:T(8,128)}, bf16[8,320,128]{2,1,0:T(8,128)(2,1)}) custom-call(bf16[128,2560]{1,0:T(8,128)(2,1)} %bitcast.14, bf16[320,1024]{1,0:T(8,128)(2,1)} %w.1, f32[1,128]{1,0:T(1,128)} %bitcast.17), custom_call_target="tpu_custom_call" | custom-call | tf_op jit(solution)/shard_map/gather/pallas_call | solution.py:657
  42.2 24.0 %attend.1 = (bf16[128,4096]{1,0:T(8,128)(2,1)}, bf16[128,4096]{1,0:T(8,128)(2,1)}, bf16[9,4,128,128]{3,2,1,0:T(8,128)(2,1)}, bf16[9,4,128,128]{3,2,1,0:T(8,128)(2,1)}, f32[1,128]{1,0:T(1,128)}) custom-call(s32[1]{0:T(128)} %bitcast.sref, s32[16,128]{1,0:T(8,128)} %bitcast.16, bf16[128,4096]{1,0:T(8,128)(2,1)} %bitcast.12, bf16[128,4096]{1,0:T(8,128)(2,1)} %bitcast.13, ...), custom_call_target="tpu_custom_call" | custom-call | tf_op jit(solution)/shard_map/attend/pallas_call | solution.py:693
  66.2 62.8 %reduce.1 = (bf16[128,2560]{1,0:T(8,128)(2,1)}, bf16[20,1024]{1,0:T(8,128)(2,1)}, f32[1,128]{1,0:T(1,128)}, f32[1,128]{1,0:T(1,128)}) custom-call(bf16[9,4,128,128]{3,2,1,0:T(8,128)(2,1)} %get-tuple-element.24.dk, bf16[9,4,128,128]{3,2,1,0:T(8,128)(2,1)} %get-tuple-element.25.dv, f32[4,128,128]{2,1,0:T(8,128)} %get-tuple-element.26.kraw, ...), custom_call_target="tpu_custom_call" | custom-call | tf_op jit(solution)/shard_map/reduce/pallas_call | solution.py:726
  129.0 0.0 copy-start
  129.0 0.0 copy-start.2
  129.1 0.0 copy-start.1
  129.1 2.0 %copy.17 = bf16[1,128,2560]{2,1,0:T(8,128)(2,1)} copy(bf16[1,128,2560]{2,1,0:T(8,128)(2,1)} %bitcast.15) | data formatting | bytes 1310720
  131.0 0.0 copy-done
  131.0 0.6 copy.18
  131.7 0.0 copy-done.2
  131.7 0.5 copy.19
  132.2 0.0 copy-done.1
  132.2 0.5 copy.20
Async XLA Ops:
  129.0 2.0 %copy-start = (bf16[20,1024]{1,0:T(8,128)(2,1)S(1)}, bf16[20,1024]{1,0:T(8,128)(2,1)}, u32[]{:S(2)}) copy-start(bf16[20,1024]{1,0:T(8,128)(2,1)} %get-tuple-element.43) | copy-start | bytes 122884
  129.0 2.6 %copy-start.2 = (f32[1,128]{1,0:T(1,128)S(1)}, f32[1,128]{1,0:T(1,128)}, u32[]{:S(2)}) copy-start(f32[1,128]{1,0:T(1,128)} %get-tuple-element.32) | copy-start | bytes 1540
  129.1 3.1 %copy-start.1 = (f32[1,128]{1,0:T(1,128)S(1)}, f32[1,128]{1,0:T(1,128)}, u32[]{:S(2)}) copy-start(f32[1,128]{1,0:T(1,128)} %get-tuple-element.33) | copy-start | bytes 1540

commit v2 on v0

v2 whole, which is shorter than its diff:
```python
import math

import jax
import jax.numpy as jnp
from jax import lax
from jax.experimental import pallas as pl
from jax.experimental.pallas import tpu as pltpu
from jax.sharding import PartitionSpec as P

MESH = pl.DeviceIdType.MESH
BF = jnp.bfloat16
F32 = jnp.float32
EPS = 1e-06
TOK = 128
HD = 128
KVH = 4
GROUP = 8
D = 2560
ROWS = 320
WIN = 9
SCALE = 1.0 / math.sqrt(HD)
LOG2E = 1.4426950408889634
NT = (((1,), (1,)), ((), ()))


class Place:
    def __init__(self):
        s = lax.axis_index("seq")
        f = lax.axis_index("fsdp")
        self.s, self.f = s, f
        self.c = lax.rem(s, 2)
        self.x = lax.rem(lax.div(s, 2), 4)
        self.yl = lax.div(s, 8)
        self.yh = lax.div(f, 4)
        self.z = lax.rem(f, 4)
        self.k = lax.div(s, 2)

    def at(self, x=None, yl=None, yh=None, z=None, c=None):
        x = self.x if x is None else x
        yl = self.yl if yl is None else yl
        yh = self.yh if yh is None else yh
        z = self.z if z is None else z
        c = self.c if c is None else c
        return ((yl * 4 + x) * 2 + c, yh * 4 + z)

    def xs(self, d):
        return lax.rem(self.x + d, 4)

    def zs(self, d):
        return lax.rem(self.z + d, 4)


class Net:
    def __init__(self, send, recv):
        self.send, self.recv, self.n = send, recv, 0
        self.sent = []

    def copy(self, src, dst, dev):
        i = self.n
        self.n += 1
        return pltpu.make_async_remote_copy(
            src_ref=src,
            dst_ref=dst,
            send_sem=self.send.at[i],
            recv_sem=self.recv.at[i],
            device_id=dev,
            device_id_type=MESH,
        )

    def start(self, copy, cond=None):
        self.sent.append((copy, cond))
        when(cond, copy.start)

    def drain(self):
        for copy, cond in self.sent:
            when(cond, copy.wait_send)


def when(cond, fn):
    if cond is None:
        fn()
    else:
        pl.when(cond)(fn)


def greet(partners):
    barrier = pltpu.get_barrier_semaphore()
    for dev in partners:
        pl.semaphore_signal(barrier, inc=1, device_id=dev, device_id_type=MESH)
    pl.semaphore_wait(barrier, len(partners))


def piece_start(i, c, z):
    return ((i // 8) * 8 + ((i // 2) % 4) * 2 + c) * 160 + ((i % 2) * 4 + z) * 20


NSEM = 160
WROWS = WIN * TOK
UNIT = 2 * TOK


def mega_kernel(
    w, hid, q, do, docs, qg, kg,
    att, dq, gh, gw, qgo, kgo,
    wbuf, hidv, hs, hT, hpk, hb, acc, kv, kraw, qv, dov, xh, rq, doT, qn, dos, w_s, ds_s, mask,
    attv, dqv, part, sb, xr, yr, t0, gb, gf, st, rbs, rbr, stf, gacc, kacc, gs1, gr1, gs2, gr2,
    send, recv, loc,
):
    p = Place()
    net = Net(send, recv)
    c, x, z, k = p.c, p.x, p.z, p.k
    row1 = p.yl == 1
    sib = p.at(c=1 - c)
    near = p.at(yl=1 - p.yl)
    far = p.at(yh=1 - p.yh, yl=1 - p.yl)
    xd = [None] + [p.at(x=p.xs(d)) for d in (1, 2, 3)]
    zd = [None] + [p.at(z=p.zs(d)) for d in (1, 2, 3)]
    fard = [None] + [p.at(yh=1 - p.yh, yl=1 - p.yl, z=p.zs(d)) for d in (1, 2, 3)]
    zgroup = [(p.zs(d), lax.rem(c + e, 2)) for d in range(4) for e in range(2)][1:]
    me16 = (p.yl * 4 + x) * 2 + p.yh
    peers = []
    for i in range(1, 16):
        o = lax.rem(me16 + i, 16)
        peers.append((o, p.at(x=lax.rem(lax.div(o, 2), 4), yl=lax.div(o, 8), yh=lax.rem(o, 2))))
    c4 = c * 4
    home, away = p.yh * 4, (1 - p.yh) * 4

    own = pl.ds(c4, 4)
    loads = []
    for n in range(8):
        j = lax.rem(c4 + n, 8)
        cols = pl.ds(pl.multiple_of(j * 128, 128), 128)
        loads.append(pltpu.make_async_copy(w.at[:, cols], wbuf.at[p.f, j], loc.at[n]))
    loads.append(pltpu.make_async_copy(hid, hidv, loc.at[8]))
    loads.append(pltpu.make_async_copy(q, qv, loc.at[9]))
    loads.append(pltpu.make_async_copy(do, dov, loc.at[10]))
    for l in loads:
        l.start()
    for m in range(1, 5):
        @pl.when(k < m)
        def _():
            kv[c, :, pl.ds((4 - m) * UNIT, UNIT), :] = jnp.zeros((KVH, UNIT, HD), BF)
    greet([p.at(z=zz, c=cc) for zz, cc in zgroup] + [d for _, d in peers] + fard[1:])
    for l in loads[:4]:
        l.wait()

    def wcopy(f, cols, dev):
        ref = wbuf.at[f, cols]
        cp = net.copy(ref, ref, dev)
        net.start(cp)
        return cp

    quarter = [None] + [wcopy(p.f, c4 + x, fard[d]) for d in (1, 2, 3)]
    first, second = pl.ds(c4, 2), pl.ds(c4 + 2, 2)
    zp0 = wcopy(p.f, first, zd[1])
    zm1 = wcopy(p.f, second, zd[3])
    far_c = wcopy(p.f, own, far)
    zp1 = wcopy(p.f, second, zd[1])
    zm0 = wcopy(p.f, first, zd[3])
    loads[8].wait()
    for f in range(8):
        hs[c, f] = hidv[:, f * ROWS:(f + 1) * ROWS]
    hs_c = net.copy(hs.at[c], hs.at[c], sib)
    net.start(hs_c)

    gain = jnp.broadcast_to(qg[...], (HD, HD)).T

    def prep(g):
        for h in range(g * GROUP, (g + 1) * GROUP):
            cols = slice(h * HD, (h + 1) * HD)
            t = qv[:, cols].astype(F32).T
            r = lax.rsqrt(jnp.mean(t * t, axis=0, keepdims=True) + EPS)
            xhat = t * r
            xh[:, cols] = xhat
            rq[:, cols] = jnp.broadcast_to(r, (8, HD))
            qn[g, :, (h % GROUP) * HD:(h % GROUP + 1) * HD] = (xhat * gain).astype(BF)
            doT[:, cols] = dov[:, cols].astype(F32).T

    loads[9].wait()
    loads[10].wait()
    prep(0)
    zp0.wait_recv()
    zpf = wcopy(home + p.zs(3), first, zd[1])
    zm1.wait_recv()
    zmf = wcopy(home + p.zs(1), second, zd[3])
    xs_c = []
    for d in (1, 3, 2):
        quarter[d].wait_recv()
        f = away + p.zs(4 - d)
        for e in (1, 3, 2):
            xs_c.append(wcopy(f, c4 + x, xd[e]))
    prep(1)

    s = p.s
    gacc[...] = jnp.zeros_like(gacc)
    kacc[...] = jnp.zeros_like(kacc)
    qd = docs[pl.ds(s, 1), :].astype(F32)
    tri = (
        lax.broadcasted_iota(jnp.int32, (TOK, TOK), 0)
        <= lax.broadcasted_iota(jnp.int32, (TOK, TOK), 1)
    )
    for d in range(WIN):
        kd = docs[pl.ds(jnp.maximum(s - d, 0), 1), :].astype(F32)
        kd = jnp.broadcast_to(kd, (TOK, TOK)).T
        live = jnp.where((kd == qd) & (s >= d), 1.0, 0.0)
        if d == 0:
            live = jnp.where(tri, live, 0.0)
        mask[pl.ds((WIN - 1 - d) * TOK, TOK), :] = live
    prep(2)
    prep(3)
    for g in range(KVH):
        for t in range(2):
            part[t, g, pl.ds(pl.multiple_of((1 - c) * WROWS, TOK), TOK), :] = jnp.zeros((TOK, HD), BF)
    for b in range(D // 128):
        hT[pl.ds(b * 128, 128), :] = hidv[:, b * 128:(b + 1) * 128].astype(F32).T
    for zc in range(4):
        for cc in range(2):
            for i in range(16):
                hpk[zc * 2 + cc, pl.ds(i * 20, 20), :] = hT[pl.ds(piece_start(i, cc, zc), 20), :].astype(BF)
    mine = z * 2 + c
    h_cps = []
    for zc, cc in zgroup:
        cp = net.copy(hpk.at[zc * 2 + cc], hb.at[mine], p.at(z=zc, c=cc))
        net.start(cp)
        h_cps.append(cp)
    own_h = pltpu.make_async_copy(hpk.at[mine], hb.at[mine], loc.at[11])
    own_h.start()

    def project(f):
        wv = jnp.concatenate([wbuf[f, c4 + n] for n in range(4)], axis=1)
        lhs = jnp.concatenate([hs[0, f], hs[1, f]], axis=0)
        return jnp.dot(lhs, wv, preferred_element_type=F32)

    hs_c.wait_recv()
    acc[...] = project(p.f)
    zp1.wait_recv()
    acc[...] += project(home + p.zs(3))
    zm0.wait_recv()
    acc[...] += project(home + p.zs(1))
    far_c.wait_recv()
    acc[...] += project(away + z)
    zpf.wait_recv()
    zmf.wait_recv()
    acc[...] += project(home + p.zs(2))
    for n, d in enumerate((1, 3, 2)):
        for e in range(3):
            xs_c[n * 3 + e].wait_recv()
        acc[...] += project(away + p.zs(4 - d))

    home_rows = pl.ds(4 * UNIT, UNIT)

    @pl.when(c == 0)
    def _():
        for g in range(KVH):
            raw = acc[:, g * HD:(g + 1) * HD]
            kraw[g] = raw
            r = lax.rsqrt(jnp.mean(raw * raw, axis=1, keepdims=True) + EPS)
            kv[0, g, home_rows, :] = (raw * r * kg[...]).astype(BF)

    @pl.when(c == 1)
    def _():
        for g in range(KVH):
            kv[1, g, home_rows, :] = acc[:, g * HD:(g + 1) * HD].astype(BF)

    def unit(m):
        return pl.ds((4 - m) * UNIT, UNIT)

    y_c, x_c, b_c = [], [], []
    for g in range(KVH):
        cp = net.copy(kv.at[c, g, unit(0)], kv.at[c, g, unit(4)], near)
        net.start(cp, p.yl == 0)
        y_c.append(cp)
        row = [None]
        for m in (1, 2, 3):
            src = kv.at[c, g, pl.ds(pl.multiple_of(jnp.where(x + m <= 3, 4 * UNIT, 0), UNIT), UNIT)]
            cp = net.copy(src, kv.at[c, g, unit(m)], xd[m])
            net.start(cp, x + m <= 3)
            row.append(cp)
        x_c.append(row)

    def spread(g):
        when(row1, y_c[g].wait_recv)
        for m in (1, 2, 3):
            net.start(x_c[g][m], row1 & (x + m > 3))

    def share(g):
        for m in (1, 2, 3):
            when(k >= m, x_c[g][m].wait_recv)
        cp = net.copy(kv.at[c, g], kv.at[c, g], sib)
        net.start(cp)
        b_c.append(cp)

    span = pl.ds(pl.multiple_of(c * TOK, TOK), WROWS)

    def open_head(g):
        b_c[g].wait_recv()
        ka = kv[0, g, span, :]
        va = kv[1, g, span, :]
        return ka, va, ka.astype(F32).T.astype(BF), va.astype(F32).T.astype(BF)

    gain2 = jnp.concatenate([gain, gain], axis=1)

    def attend(g, pair, head):
        ka, va, kT, vT = head
        lo = pair * 256
        cols = slice(lo, lo + 256)
        full = slice(g * 1024 + lo, g * 1024 + lo + 256)
        scores = jnp.dot(ka, qn[g, :, cols], preferred_element_type=F32)
        m = mask[...]
        e = jnp.exp2(scores * (SCALE * LOG2E)) * jnp.concatenate([m, m], axis=1)
        total = jnp.sum(e, axis=0, keepdims=True)
        wt = e.astype(BF)
        w_s[:, cols] = wt
        inv = 1.0 / total
        d_out = doT[:, full]
        attT = (jnp.dot(vT, wt, preferred_element_type=F32) * inv).astype(BF).astype(F32)
        delta = jnp.sum(d_out * attT, axis=0, keepdims=True) * inv
        dsc = (d_out * inv).astype(BF)
        dos[:, cols] = dsc
        dp = jnp.dot(va, dsc, preferred_element_type=F32)
        ds = (e * (dp - delta)).astype(BF)
        ds_s[:, cols] = ds
        dy = jnp.dot(kT, ds, preferred_element_type=F32) * SCALE
        xhat = xh[:, full]
        r = rq[0:1, full]
        gacc[...] += dy * xhat
        dxh = dy * gain2
        dx = r * (dxh - xhat * jnp.mean(xhat * dxh, axis=0, keepdims=True))
        for n in range(2):
            at = slice(g * 1024 + lo + n * HD, g * 1024 + lo + (n + 1) * HD)
            attv[:, at] = attT[:, n * HD:(n + 1) * HD].T.astype(BF)
            dqv[:, at] = dx[:, n * HD:(n + 1) * HD].T.astype(BF)

    outs = []

    def close_head(g):
        dvv = lax.dot_general(w_s[...], dos[...], NT, preferred_element_type=F32)
        part[1, g, span, :] = dvv.astype(BF)
        dkk = lax.dot_general(ds_s[...], qn[g], NT, preferred_element_type=F32) * SCALE
        part[0, g, span, :] = dkk.astype(BF)
        cols = pl.ds(g * 1024, 1024)
        for n, (a, b) in enumerate(((attv, att), (dqv, dq))):
            cp = pltpu.make_async_copy(a.at[:, cols], b.at[:, cols], loc.at[12 + g * 2 + n])
            cp.start()
            outs.append(cp)

    s_c, u_c, v_c, z_c, w_c = {}, {}, {}, {}, {}

    def c1(g):
        s_c[g] = net.copy(part.at[1 - c, g], sb.at[g], sib)
        net.start(s_c[g])

    def c2(g):
        s_c[g].wait_recv()
        part[c, g] = (part[c, g].astype(F32) + sb[g].astype(F32)).astype(BF)
        u_c[g] = [None]
        for m in (1, 2, 3):
            cp = net.copy(part.at[c, g, unit(m)], xr.at[g, m - 1], xd[4 - m])
            net.start(cp, k >= m)
            u_c[g].append(cp)

    def c3(g):
        t0[...] = part[c, g, unit(0), :].astype(F32)
        for m in (1, 2, 3):
            @pl.when(x + m <= 3)
            def _():
                u_c[g][m].wait_recv()
                t0[...] += xr[g, m - 1].astype(F32)

            @pl.when((x + m > 3) & row1)
            def _():
                u_c[g][m].wait_recv()
                part[c, g, unit(4), :] = (
                    part[c, g, unit(4), :].astype(F32) + xr[g, m - 1].astype(F32)
                ).astype(BF)

        v_c[g] = net.copy(part.at[c, g, unit(4)], yr.at[g], near)
        net.start(v_c[g], row1)
        part[c, g, unit(0), :] = t0[...].astype(BF)

    def c4(g):
        t0[...] = part[c, g, unit(0), :].astype(F32)

        @pl.when(p.yl == 0)
        def _():
            v_c[g].wait_recv()
            t0[...] += yr[g].astype(F32)

        @pl.when(c == 0)
        def _():
            raw = kraw[g]
            r = lax.rsqrt(jnp.mean(raw * raw, axis=1, keepdims=True) + EPS)
            xhat = raw * r
            dy = t0[...]
            kacc[...] += jnp.sum(dy * xhat, axis=0, keepdims=True)
            dxh = dy * kg[...]
            dx = r * (dxh - xhat * jnp.mean(xhat * dxh, axis=1, keepdims=True))
            gb[0, g, z] = dx.astype(BF)

        @pl.when(c == 1)
        def _():
            gb[1, g, z] = t0[...].astype(BF)

        z_c[g] = []
        for d in (1, 3, 2):
            cp = net.copy(gb.at[c, g, z], gb.at[c, g, z], zd[d])
            net.start(cp)
            z_c[g].append(cp)

    def d1(g):
        for cp in z_c[g]:
            cp.wait_recv()
        w_c[g] = net.copy(gb.at[c, g], gb.at[c, g], sib)
        net.start(w_c[g])

    def weight_terms(g):
        w_c[g].wait_recv()
        lhs = jnp.concatenate([hb[i] for i in range(8)], axis=1)
        rhs = jnp.concatenate([gb[0, g].reshape(8 * TOK, HD), gb[1, g].reshape(8 * TOK, HD)], axis=1)
        gf[...] = jnp.dot(lhs, rhs, preferred_element_type=F32)
        for i in range(16):
            for t in range(2):
                st[i, pl.ds(((g % 2) * 2 + t) * 20, 20), :] = gf[pl.ds(i * 20, 20), t * HD:(t + 1) * HD]

    r_c = []

    def scatter(n):
        for i in range(16):
            rbs[n, i] = st[i].astype(BF)
        row = []
        for o, dev in peers:
            cp = net.copy(rbs.at[n, o], rbr.at[n, me16], dev)
            net.start(cp)
            row.append(cp)
        r_c.append(row)
        rbr[n, me16] = rbs[n, me16]

    def collect(n):
        for cp in r_c[n]:
            cp.wait_recv()
        total = rbr[n, 0].astype(F32)
        for i in range(1, 16):
            total = total + rbr[n, i].astype(F32)
        stf[...] = total
        for b in range(2):
            for t in range(2):
                at = (t * 4 + n * 2 + b) * HD
                gw[:, at:at + HD] = stf[pl.ds((b * 2 + t) * 20, 20), :].astype(BF)

    spread(0)
    spread(1)
    share(0)

    w_sib = []

    def weight_share():
        for f in (home + p.zs(1), home + p.zs(2), home + p.zs(3), away, away + 1, away + 2, away + 3):
            w_sib.append(wcopy(f, own, sib))

    todo = {
        0: [lambda: spread(2), lambda: share(1)],
        1: [lambda: spread(3), weight_share],
        2: [lambda: share(2)],
        3: [lambda: c1(0), lambda: share(3)],
        5: [lambda: c2(0)],
        7: [lambda: c1(1)],
        8: [lambda: c3(0)],
        9: [lambda: c2(1)],
        10: [lambda: c4(0)],
        11: [lambda: c1(2)],
        12: [lambda: c3(1), lambda: d1(0)],
        13: [lambda: c2(2)],
        14: [lambda: c4(1)],
        15: [lambda: c1(3)],
    }
    for g in range(KVH):
        head = open_head(g)
        for pair in range(4):
            attend(g, pair, head)
            if pair == 3:
                close_head(g)
            for fn in todo.get(g * 4 + pair, ()):
                fn()

    c3(2)
    d1(1)
    c2(3)
    for cp in h_cps:
        cp.wait_recv()
    own_h.wait()
    c4(2)
    weight_terms(0)
    c3(3)
    weight_terms(1)
    scatter(0)
    d1(2)
    c4(3)
    a = gacc[:, :HD] + gacc[:, HD:]
    gs1[...] = jnp.concatenate(
        [jnp.sum(a.T, axis=0, keepdims=True), kacc[...], jnp.zeros((6, HD), F32)], axis=0
    )
    g1 = []
    for zc, cc in zgroup:
        cp = net.copy(gs1, gr1.at[mine], p.at(z=zc, c=cc))
        net.start(cp)
        g1.append(cp)
    gr1[mine] = gs1[...]
    weight_terms(2)
    d1(3)
    for cp in g1:
        cp.wait_recv()
    gs2[...] = jnp.sum(gr1[...], axis=0)
    g2 = []
    for o, dev in peers:
        cp = net.copy(gs2, gr2.at[me16], dev)
        net.start(cp)
        g2.append(cp)
    gr2[me16] = gs2[...]
    weight_terms(3)
    scatter(1)

    for l in loads[4:8]:
        l.wait()
    for cp in w_sib:
        cp.wait_recv()
    tokens = pl.ds(pl.multiple_of(c * TOK, TOK), TOK)
    gkv = jnp.concatenate([gb[t, g, z, tokens, :] for t in range(2) for g in range(KVH)], axis=1)
    for f in range(8):
        wv = jnp.concatenate([wbuf[f, j] for j in range(8)], axis=1)
        gh[:, f * ROWS:(f + 1) * ROWS] = lax.dot_general(
            gkv, wv, NT, preferred_element_type=F32
        ).astype(BF)
    collect(0)
    for cp in g2:
        cp.wait_recv()
    gsum = jnp.sum(gr2[...], axis=0)
    qgo[...] = gsum[0:1]
    kgo[...] = gsum[1:2]
    for cp in outs:
        cp.wait()
    collect(1)
    net.drain()
    assert net.n <= NSEM


def shards(hidden, queries, doc_ids, kv_weight, q_gain, k_gain, grad_out):
    vm = pl.BlockSpec(memory_space=pltpu.VMEM)
    hbm = pl.BlockSpec(memory_space=pl.ANY)
    sds = jax.ShapeDtypeStruct
    vmem = pltpu.VMEM
    wide = QW = 32 * HD
    att, dq, gh, gw, qgo, kgo = pl.pallas_call(
        mega_kernel,
        out_shape=(
            sds((TOK, QW), BF),
            sds((TOK, QW), BF),
            sds((TOK, D), BF),
            sds((20, 1024), BF),
            sds((1, HD), F32),
            sds((1, HD), F32),
        ),
        in_specs=[hbm, hbm, hbm, hbm, vm, vm, vm],
        out_specs=(hbm, hbm, vm, vm, vm, vm),
        scratch_shapes=[
            vmem((8, 8, ROWS, 128), BF),
            vmem((TOK, D), BF),
            vmem((2, 8, TOK, ROWS), BF),
            vmem((D, TOK), F32),
            vmem((8, ROWS, TOK), BF),
            vmem((8, ROWS, TOK), BF),
            vmem((UNIT, 512), F32),
            vmem((2, KVH, 5 * UNIT, HD), BF),
            vmem((KVH, UNIT, HD), F32),
            vmem((TOK, wide), BF),
            vmem((TOK, wide), BF),
            vmem((HD, wide), F32),
            vmem((8, wide), F32),
            vmem((HD, wide), F32),
            vmem((KVH, HD, GROUP * TOK), BF),
            vmem((HD, GROUP * TOK), BF),
            vmem((WROWS, GROUP * TOK), BF),
            vmem((WROWS, GROUP * TOK), BF),
            vmem((WROWS, TOK), F32),
            vmem((TOK, wide), BF),
            vmem((TOK, wide), BF),
            vmem((2, KVH, 5 * UNIT, HD), BF),
            vmem((KVH, 5 * UNIT, HD), BF),
            vmem((KVH, 3, UNIT, HD), BF),
            vmem((KVH, UNIT, HD), BF),
            vmem((UNIT, HD), F32),
            vmem((2, KVH, 4, UNIT, HD), BF),
            vmem((ROWS, 2 * HD), F32),
            vmem((16, 80, HD), F32),
            vmem((2, 16, 80, HD), BF),
            vmem((2, 16, 80, HD), BF),
            vmem((80, HD), F32),
            vmem((HD, 256), F32),
            vmem((1, HD), F32),
            vmem((8, HD), F32),
            vmem((8, 8, HD), F32),
            vmem((8, HD), F32),
            vmem((16, 8, HD), F32),
            pltpu.SemaphoreType.DMA((NSEM,)),
            pltpu.SemaphoreType.DMA((NSEM,)),
            pltpu.SemaphoreType.DMA((20,)),
        ],
        compiler_params=pltpu.CompilerParams(
            collective_id=0, has_side_effects=True, vmem_limit_bytes=60 * 1024 * 1024
        ),
        name="mega",
    )(
        kv_weight, hidden[0], queries[0], grad_out[0], doc_ids[0].reshape(16, TOK),
        q_gain.reshape(1, HD), k_gain.reshape(1, HD),
    )
    return (att[None], dq[None], gh[None], gw, qgo.reshape(HD), kgo.reshape(HD))


def solution(mesh):
    return jax.shard_map(
        shards,
        mesh=mesh,
        in_specs=(
            P("fsdp", "seq", None),
            P("fsdp", "seq", None),
            P("fsdp", None),
            P("fsdp", None),
            P(),
            P(),
            P("fsdp", "seq", None),
        ),
        out_specs=(
            P("fsdp", "seq", None),
            P("fsdp", "seq", None),
            P("fsdp", "seq", None),
            P(("seq", "fsdp"), None),
            P(),
            P(),
        ),
        check_vma=False,
    )
```

time: 470 us -> 109 us (0.23)
  waiting for transfers between devices: 212 us -> 0 us
  blocking collectives: 120 us -> 0 us
  Pallas kernels: 0 us -> 101 us
  local copies, waits for them, and re-layouts: 56.5 us -> 6.48 us
  matrix products: 29.8 us -> 0 us
  other arithmetic: 27.3 us -> 0 us
  between operations: 14.1 us -> 0.66 us
  loops' own time: 8.37 us -> 0 us
    all_gather x3 -> x0, waiting for transfers between devices: 139 us -> none  [the longest x1 84.9 us: shards(): lax.all_gather(kv_weight, 'fsdp', axis=0, tiled=True)]
    unnamed x1 -> x0, blocking collectives: 120 us -> none
    pallas_call x0 -> x1, Pallas kernels: none -> 101 us  [shards(): pl.pallas_call(mega_kernel, out_shape=(sds((TOK, QW), BF), sds((TOK, QW),...]
    reduce_scatter x1 -> x0, waiting for transfers between devices: 72.6 us -> none  [shards(): lax.psum_scatter(key_terms.reshape(pack, 2 * kv_width).astype(jnp.bfloat1...]
    dot_general x10 -> x0, matrix products: 29.8 us -> none  [the longest x1 5.55 us: shards(): jnp.einsum('tr,tk->rk', tokens, grad_kv, preferred_element_type=jnp.float32)]
    reduce_sum x8 -> x0, other arithmetic: 11.6 us -> none  [the longest x5 6.06 us: normalize(): values * lax.rsqrt(jnp.mean(values * values, axis=-1, keepdims=True) + ep...]
    another operation x10 -> x0, loops' own time: 8.37 us -> none  [the longest x1 5.47 us: shards(): lax.scan(backward_block, jnp.zeros((tok_dev, kv_heads, group, head_dim),...]
    unnamed x58 -> x16, local copies, waits for them, and re-layouts: 14.2 us -> 6.48 us
  transfers between devices with their start and end apart: 4 -> 0, of which waited for: 4 -> 0; matrix products, arithmetic and copies ran while one was open for 9% -> 0% of each run, Pallas kernels for 0% -> 0%
where the time goes in v2:
time: 109 us; the launch traced here: 108 us
  Pallas kernels  101 us (93%)
  local copies, waits for them, and re-layouts  6.48 us (6%)
    pallas_call x1, Pallas kernels, shards(): pl.pallas_call(mega_kernel, out_shape=(sds((TOK, QW), BF), sds((TOK, QW),...  101 us
    unnamed x16, local copies, waits for them, and re-layouts  6.48 us

profile of v2, /device:TPU:1, one launch (start us, length us, event | category | flops | bytes accessed | tf_op | source)
XLA Modules:
  0.0 108.4 jit_solution(12790516615021860809)
XLA Ops:
  0.6 101.2 %mega.1 = (bf16[128,4096]{1,0:T(8,128)(2,1)}, bf16[128,4096]{1,0:T(8,128)(2,1)}, bf16[128,2560]{1,0:T(8,128)(2,1)}, bf16[20,1024]{1,0:T(8,128)(2,1)}, f32[1,128]{1,0:T(1,128)}, /*index=5*/f32[1,128]{1,0:T(1,128)}) custom-call(bf16[320,1024]{1,0:T(8,128)(2,1)} %w.1, bf16[128,2560]{1,0:T(8,128)(2,1)} %bitcast.16, bf16[128,4096]{1,0:T(8,128)(2,1)} %bitcast.11, ...), custom_call_target="tpu_custom_call" | custom-call | tf_op jit(solution)/shard_map/mega/pallas_call | solution.py:552
  101.9 0.0 copy-start
  101.9 2.4 %copy.19 = bf16[1,128,4096]{2,1,0:T(8,128)(2,1)} copy(bf16[1,128,4096]{2,1,0:T(8,128)(2,1)} %bitcast.14) | data formatting | bytes 2097152
  104.3 0.0 copy-done
  104.3 0.0 copy-start.1
  104.3 1.0 copy.20
  105.3 0.5 copy-done.1
  105.7 0.0 copy-start.2
  105.7 0.8 copy.21
  106.6 0.0 copy-done.2
  106.6 0.0 copy-start.4
  106.6 0.6 copy.22
  107.2 0.0 copy-done.4
  107.2 0.0 copy-start.3
  107.2 0.5 copy.23
  107.7 0.1 copy-done.3
  107.9 0.5 copy.24
Async XLA Ops:
  101.9 2.4 %copy-start = (bf16[128,4096]{1,0:T(8,128)(2,1)S(1)}, bf16[128,4096]{1,0:T(8,128)(2,1)}, u32[]{:S(2)}) copy-start(bf16[128,4096]{1,0:T(8,128)(2,1)} %get-tuple-element.13) | copy-start | bytes 3145732
  104.3 1.5 %copy-start.1 = (bf16[128,2560]{1,0:T(8,128)(2,1)S(1)}, bf16[128,2560]{1,0:T(8,128)(2,1)}, u32[]{:S(2)}) copy-start(bf16[128,2560]{1,0:T(8,128)(2,1)} %get-tuple-element.14) | copy-start | bytes 1966084
  105.7 0.8 copy-start.2
  106.6 0.6 copy-start.4
  107.2 0.7 copy-start.3

commit v3 on v2

--- a/solution.py
+++ b/solution.py
@@ -94,16 +94,18 @@
     return ((i // 8) * 8 + ((i // 2) % 4) * 2 + c) * 160 + ((i % 2) * 4 + z) * 20
 
 
-NSEM = 160
+NSEM = 208
 WROWS = WIN * TOK
 UNIT = 2 * TOK
+CUTS = (pl.ds(0, 128), pl.ds(128, 48))
+HEADS = ((0, 1, 2), (3,))
 
 
 def mega_kernel(
     w, hid, q, do, docs, qg, kg,
     att, dq, gh, gw, qgo, kgo,
-    wbuf, hidv, hs, hT, hpk, hb, acc, kv, kraw, qv, dov, xh, rq, doT, qn, dos, w_s, ds_s, mask,
-    attv, dqv, part, sb, xr, yr, t0, gb, gf, st, rbs, rbr, stf, gacc, kacc, gs1, gr1, gs2, gr2,
+    wbuf, hidv, hT, hpk, hb, kv, kraw, qv, dov, xh, rq, doT, qn, dos, w_s, ds_s, mask,
+    attv, dqv, ghv, part, sb, xr, yr, t0, gb, gf, st, rbs, rbr, stf, gacc, kacc, gs1, gr1, gs2, gr2,
     send, recv, loc,
 ):
     p = Place()
@@ -122,16 +124,16 @@
     for i in range(1, 16):
         o = lax.rem(me16 + i, 16)
         peers.append((o, p.at(x=lax.rem(lax.div(o, 2), 4), yl=lax.div(o, 8), yh=lax.rem(o, 2))))
-    c4 = c * 4
+    cj = c * 4
     home, away = p.yh * 4, (1 - p.yh) * 4
 
-    own = pl.ds(c4, 4)
+    own = pl.ds(cj, 4)
     loads = []
     for n in range(8):
-        j = lax.rem(c4 + n, 8)
+        j = lax.rem(cj + n, 8)
         cols = pl.ds(pl.multiple_of(j * 128, 128), 128)
         loads.append(pltpu.make_async_copy(w.at[:, cols], wbuf.at[p.f, j], loc.at[n]))
-    loads.append(pltpu.make_async_copy(hid, hidv, loc.at[8]))
+    loads.append(pltpu.make_async_copy(hid, hidv.at[c], loc.at[8]))
     loads.append(pltpu.make_async_copy(q, qv, loc.at[9]))
     loads.append(pltpu.make_async_copy(do, dov, loc.at[10]))
     for l in loads:
@@ -144,24 +146,42 @@
     for l in loads[:4]:
         l.wait()
 
-    def wcopy(f, cols, dev):
-        ref = wbuf.at[f, cols]
+    def wcopy(f, j, lo, n, dev):
+        ref = wbuf.at[f, j, pl.ds(lo, n)]
         cp = net.copy(ref, ref, dev)
         net.start(cp)
         return cp
 
-    quarter = [None] + [wcopy(p.f, c4 + x, fard[d]) for d in (1, 2, 3)]
-    first, second = pl.ds(c4, 2), pl.ds(c4 + 2, 2)
-    zp0 = wcopy(p.f, first, zd[1])
-    zm1 = wcopy(p.f, second, zd[3])
-    far_c = wcopy(p.f, own, far)
-    zp1 = wcopy(p.f, second, zd[1])
-    zm0 = wcopy(p.f, first, zd[3])
+    half, fourth = ROWS // 2, ROWS // 4
+    mine4 = pl.multiple_of(x * fourth, 16)
+    quarter, zp0, zp1, zm0, zm1, far_c, zpf, zmf, xs_c = ([None] * KVH for _ in range(9))
+
+    def push(g):
+        j = cj + g
+        quarter[g] = [None] + [wcopy(p.f, j, mine4, fourth, fard[d]) for d in (1, 2, 3)]
+        zp0[g] = wcopy(p.f, j, 0, half, zd[1])
+        zm1[g] = wcopy(p.f, j, half, half, zd[3])
+        far_c[g] = wcopy(p.f, j, 0, ROWS, far)
+        zp1[g] = wcopy(p.f, j, half, half, zd[1])
+        zm0[g] = wcopy(p.f, j, 0, half, zd[3])
+
+    def relay(g):
+        j = cj + g
+        zp0[g].wait_recv()
+        zpf[g] = wcopy(home + p.zs(3), j, 0, half, zd[1])
+        zm1[g].wait_recv()
+        zmf[g] = wcopy(home + p.zs(1), j, half, half, zd[3])
+        xs_c[g] = []
+        for d in (1, 3, 2):
+            quarter[g][d].wait_recv()
+            for e in (1, 3, 2):
+                xs_c[g].append(wcopy(away + p.zs(4 - d), j, mine4, fourth, xd[e]))
+
+    push(0)
     loads[8].wait()
-    for f in range(8):
-        hs[c, f] = hidv[:, f * ROWS:(f + 1) * ROWS]
-    hs_c = net.copy(hs.at[c], hs.at[c], sib)
+    hs_c = net.copy(hidv.at[c], hidv.at[c], sib)
     net.start(hs_c)
+    push(1)
 
     gain = jnp.broadcast_to(qg[...], (HD, HD)).T
 
@@ -179,94 +199,77 @@
     loads[9].wait()
     loads[10].wait()
     prep(0)
-    zp0.wait_recv()
-    zpf = wcopy(home + p.zs(3), first, zd[1])
-    zm1.wait_recv()
-    zmf = wcopy(home + p.zs(1), second, zd[3])
-    xs_c = []
-    for d in (1, 3, 2):
-        quarter[d].wait_recv()
-        f = away + p.zs(4 - d)
-        for e in (1, 3, 2):
-            xs_c.append(wcopy(f, c4 + x, xd[e]))
+    relay(0)
+    push(2)
     prep(1)
-
-    s = p.s
-    gacc[...] = jnp.zeros_like(gacc)
-    kacc[...] = jnp.zeros_like(kacc)
-    qd = docs[pl.ds(s, 1), :].astype(F32)
-    tri = (
-        lax.broadcasted_iota(jnp.int32, (TOK, TOK), 0)
-        <= lax.broadcasted_iota(jnp.int32, (TOK, TOK), 1)
-    )
-    for d in range(WIN):
-        kd = docs[pl.ds(jnp.maximum(s - d, 0), 1), :].astype(F32)
-        kd = jnp.broadcast_to(kd, (TOK, TOK)).T
-        live = jnp.where((kd == qd) & (s >= d), 1.0, 0.0)
-        if d == 0:
-            live = jnp.where(tri, live, 0.0)
-        mask[pl.ds((WIN - 1 - d) * TOK, TOK), :] = live
+    relay(1)
+    push(3)
     prep(2)
-    prep(3)
-    for g in range(KVH):
-        for t in range(2):
-            part[t, g, pl.ds(pl.multiple_of((1 - c) * WROWS, TOK), TOK), :] = jnp.zeros((TOK, HD), BF)
-    for b in range(D // 128):
-        hT[pl.ds(b * 128, 128), :] = hidv[:, b * 128:(b + 1) * 128].astype(F32).T
-    for zc in range(4):
-        for cc in range(2):
-            for i in range(16):
-                hpk[zc * 2 + cc, pl.ds(i * 20, 20), :] = hT[pl.ds(piece_start(i, cc, zc), 20), :].astype(BF)
+
+    def window_mask():
+        qd = docs[pl.ds(p.s, 1), :].astype(F32)
+        tri = (
+            lax.broadcasted_iota(jnp.int32, (TOK, TOK), 0)
+            <= lax.broadcasted_iota(jnp.int32, (TOK, TOK), 1)
+        )
+        for d in range(WIN):
+            kd = docs[pl.ds(jnp.maximum(p.s - d, 0), 1), :].astype(F32)
+            kd = jnp.broadcast_to(kd, (TOK, TOK)).T
+            live = jnp.where((kd == qd) & (p.s >= d), 1.0, 0.0)
+            if d == 0:
+                live = jnp.where(tri, live, 0.0)
+            mask[pl.ds((WIN - 1 - d) * TOK, TOK), :] = live
+
+    def clear():
+        gacc[...] = jnp.zeros_like(gacc)
+        kacc[...] = jnp.zeros_like(kacc)
+        st[...] = jnp.zeros_like(st)
+        for g in range(KVH):
+            for t in range(2):
+                part[t, g, pl.ds(pl.multiple_of((1 - c) * WROWS, TOK), TOK), :] = jnp.zeros((TOK, HD), BF)
+
     mine = z * 2 + c
     h_cps = []
-    for zc, cc in zgroup:
-        cp = net.copy(hpk.at[zc * 2 + cc], hb.at[mine], p.at(z=zc, c=cc))
-        net.start(cp)
-        h_cps.append(cp)
     own_h = pltpu.make_async_copy(hpk.at[mine], hb.at[mine], loc.at[11])
-    own_h.start()
-
-    def project(f):
-        wv = jnp.concatenate([wbuf[f, c4 + n] for n in range(4)], axis=1)
-        lhs = jnp.concatenate([hs[0, f], hs[1, f]], axis=0)
-        return jnp.dot(lhs, wv, preferred_element_type=F32)
-
-    hs_c.wait_recv()
-    acc[...] = project(p.f)
-    zp1.wait_recv()
-    acc[...] += project(home + p.zs(3))
-    zm0.wait_recv()
-    acc[...] += project(home + p.zs(1))
-    far_c.wait_recv()
-    acc[...] += project(away + z)
-    zpf.wait_recv()
-    zmf.wait_recv()
-    acc[...] += project(home + p.zs(2))
-    for n, d in enumerate((1, 3, 2)):
-        for e in range(3):
-            xs_c[n * 3 + e].wait_recv()
-        acc[...] += project(away + p.zs(4 - d))
+
+    def exchange_hidden():
+        for b in range(D // 128):
+            hT[pl.ds(b * 128, 128), :] = hidv[c, :, b * 128:(b + 1) * 128].astype(F32).T
+        for zc in range(4):
+            for cc in range(2):
+                for i in range(16):
+                    hpk[zc * 2 + cc, pl.ds(i * 20, 20), :] = hT[pl.ds(piece_start(i, cc, zc), 20), :].astype(BF)
+        for zc, cc in zgroup:
+            cp = net.copy(hpk.at[zc * 2 + cc], hb.at[mine], p.at(z=zc, c=cc))
+            net.start(cp)
+            h_cps.append(cp)
+        own_h.start()
 
     home_rows = pl.ds(4 * UNIT, UNIT)
 
-    @pl.when(c == 0)
-    def _():
-        for g in range(KVH):
-            raw = acc[:, g * HD:(g + 1) * HD]
+    def unit(m):
+        return pl.ds((4 - m) * UNIT, UNIT)
+
+    y_c, x_c, b_c = [], [], []
+
+    def project(g):
+        if g == 0:
+            hs_c.wait_recv()
+        for cp in (zp1[g], zm0[g], far_c[g], zpf[g], zmf[g], *xs_c[g]):
+            cp.wait_recv()
+        lhs = jnp.concatenate([hidv[0], hidv[1]], axis=0)
+        raw = jnp.dot(lhs, wbuf[:, cj + g].reshape(D, 128), preferred_element_type=F32)
+
+        @pl.when(c == 0)
+        def _():
             kraw[g] = raw
             r = lax.rsqrt(jnp.mean(raw * raw, axis=1, keepdims=True) + EPS)
             kv[0, g, home_rows, :] = (raw * r * kg[...]).astype(BF)
 
-    @pl.when(c == 1)
-    def _():
-        for g in range(KVH):
-            kv[1, g, home_rows, :] = acc[:, g * HD:(g + 1) * HD].astype(BF)
-
-    def unit(m):
-        return pl.ds((4 - m) * UNIT, UNIT)
-
-    y_c, x_c, b_c = [], [], []
-    for g in range(KVH):
+        @pl.when(c == 1)
+        def _():
+            kv[1, g, home_rows, :] = raw.astype(BF)
+
         cp = net.copy(kv.at[c, g, unit(0)], kv.at[c, g, unit(4)], near)
         net.start(cp, p.yl == 0)
         y_c.append(cp)
@@ -413,6 +416,9 @@
         w_c[g] = net.copy(gb.at[c, g], gb.at[c, g], sib)
         net.start(w_c[g])
 
+    def offset(g, t):
+        return (g * 2 + t) * 20 + (8 if g == 3 else 0)
+
     def weight_terms(g):
         w_c[g].wait_recv()
         lhs = jnp.concatenate([hb[i] for i in range(8)], axis=1)
@@ -420,58 +426,71 @@
         gf[...] = jnp.dot(lhs, rhs, preferred_element_type=F32)
         for i in range(16):
             for t in range(2):
-                st[i, pl.ds(((g % 2) * 2 + t) * 20, 20), :] = gf[pl.ds(i * 20, 20), t * HD:(t + 1) * HD]
+                st[i, pl.ds(offset(g, t), 20), :] = gf[pl.ds(i * 20, 20), t * HD:(t + 1) * HD]
 
     r_c = []
 
     def scatter(n):
+        rows = CUTS[n]
         for i in range(16):
-            rbs[n, i] = st[i].astype(BF)
+            rbs[i, rows] = st[i, rows].astype(BF)
         row = []
         for o, dev in peers:
-            cp = net.copy(rbs.at[n, o], rbr.at[n, me16], dev)
+            cp = net.copy(rbs.at[o, rows], rbr.at[me16, rows], dev)
             net.start(cp)
             row.append(cp)
         r_c.append(row)
-        rbr[n, me16] = rbs[n, me16]
+        rbr[me16, rows] = rbs[me16, rows]
 
     def collect(n):
+        rows = CUTS[n]
         for cp in r_c[n]:
             cp.wait_recv()
-        total = rbr[n, 0].astype(F32)
+        total = rbr[0, rows].astype(F32)
         for i in range(1, 16):
-            total = total + rbr[n, i].astype(F32)
-        stf[...] = total
-        for b in range(2):
+            total = total + rbr[i, rows].astype(F32)
+        stf[rows] = total
+        for g in HEADS[n]:
             for t in range(2):
-                at = (t * 4 + n * 2 + b) * HD
-                gw[:, at:at + HD] = stf[pl.ds((b * 2 + t) * 20, 20), :].astype(BF)
-
-    spread(0)
-    spread(1)
-    share(0)
+                at = (t * 4 + g) * HD
+                gw[:, at:at + HD] = stf[pl.ds(offset(g, t), 20), :].astype(BF)
 
     w_sib = []
 
     def weight_share():
         for f in (home + p.zs(1), home + p.zs(2), home + p.zs(3), away, away + 1, away + 2, away + 3):
-            w_sib.append(wcopy(f, own, sib))
+            ref = wbuf.at[f, own]
+            cp = net.copy(ref, ref, sib)
+            net.start(cp)
+            w_sib.append(cp)
+
+    project(0)
+    relay(2)
+    project(1)
+    prep(3)
+    relay(3)
+    spread(0)
+    window_mask()
+    clear()
+    project(2)
+    spread(1)
+    exchange_hidden()
+    share(0)
+    project(3)
+    spread(2)
 
     todo = {
-        0: [lambda: spread(2), lambda: share(1)],
-        1: [lambda: spread(3), weight_share],
-        2: [lambda: share(2)],
-        3: [lambda: c1(0), lambda: share(3)],
-        5: [lambda: c2(0)],
+        0: [lambda: share(1)],
+        1: [lambda: spread(3)],
+        2: [lambda: share(2), weight_share],
+        3: [lambda: c1(0)],
+        5: [lambda: share(3)],
+        6: [lambda: c2(0)],
         7: [lambda: c1(1)],
-        8: [lambda: c3(0)],
-        9: [lambda: c2(1)],
-        10: [lambda: c4(0)],
-        11: [lambda: c1(2)],
-        12: [lambda: c3(1), lambda: d1(0)],
-        13: [lambda: c2(2)],
-        14: [lambda: c4(1)],
-        15: [lambda: c1(3)],
+        10: [lambda: c2(1)],
+        11: [lambda: c3(0), lambda: c1(2)],
+        14: [lambda: c2(2)],
+        15: [lambda: c1(3), lambda: c4(0)],
     }
     for g in range(KVH):
         head = open_head(g)
@@ -482,18 +501,19 @@
             for fn in todo.get(g * 4 + pair, ()):
                 fn()
 
-    c3(2)
-    d1(1)
+    c3(1)
     c2(3)
     for cp in h_cps:
         cp.wait_recv()
     own_h.wait()
-    c4(2)
+    d1(0)
+    c3(2)
+    c4(1)
     weight_terms(0)
     c3(3)
+    d1(1)
+    c4(2)
     weight_terms(1)
-    scatter(0)
-    d1(2)
     c4(3)
     a = gacc[:, :HD] + gacc[:, HD:]
     gs1[...] = jnp.concatenate(
@@ -505,7 +525,9 @@
         net.start(cp)
         g1.append(cp)
     gr1[mine] = gs1[...]
+    d1(2)
     weight_terms(2)
+    scatter(0)
     d1(3)
     for cp in g1:
         cp.wait_recv()
@@ -527,9 +549,12 @@
     gkv = jnp.concatenate([gb[t, g, z, tokens, :] for t in range(2) for g in range(KVH)], axis=1)
     for f in range(8):
         wv = jnp.concatenate([wbuf[f, j] for j in range(8)], axis=1)
-        gh[:, f * ROWS:(f + 1) * ROWS] = lax.dot_general(
+        ghv[:, f * ROWS:(f + 1) * ROWS] = lax.dot_general(
             gkv, wv, NT, preferred_element_type=F32
         ).astype(BF)
+    cp = pltpu.make_async_copy(ghv, gh, loc.at[4])
+    cp.start()
+    outs.append(cp)
     collect(0)
     for cp in g2:
         cp.wait_recv()
@@ -543,32 +568,36 @@
     assert net.n <= NSEM
 
 
+def finish_kernel(*refs):
+    n = len(refs) // 2
+    for a, b in zip(refs[:n], refs[n:]):
+        b[...] = a[...]
+
+
 def shards(hidden, queries, doc_ids, kv_weight, q_gain, k_gain, grad_out):
     vm = pl.BlockSpec(memory_space=pltpu.VMEM)
     hbm = pl.BlockSpec(memory_space=pl.ANY)
     sds = jax.ShapeDtypeStruct
     vmem = pltpu.VMEM
-    wide = QW = 32 * HD
+    wide = 32 * HD
     att, dq, gh, gw, qgo, kgo = pl.pallas_call(
         mega_kernel,
         out_shape=(
-            sds((TOK, QW), BF),
-            sds((TOK, QW), BF),
+            sds((TOK, wide), BF),
+            sds((TOK, wide), BF),
             sds((TOK, D), BF),
             sds((20, 1024), BF),
             sds((1, HD), F32),
             sds((1, HD), F32),
         ),
         in_specs=[hbm, hbm, hbm, hbm, vm, vm, vm],
-        out_specs=(hbm, hbm, vm, vm, vm, vm),
+        out_specs=(hbm, hbm, hbm, vm, vm, vm),
         scratch_shapes=[
             vmem((8, 8, ROWS, 128), BF),
-            vmem((TOK, D), BF),
-            vmem((2, 8, TOK, ROWS), BF),
+            vmem((2, TOK, D), BF),
             vmem((D, TOK), F32),
             vmem((8, ROWS, TOK), BF),
             vmem((8, ROWS, TOK), BF),
-            vmem((UNIT, 512), F32),
             vmem((2, KVH, 5 * UNIT, HD), BF),
             vmem((KVH, UNIT, HD), F32),
             vmem((TOK, wide), BF),
@@ -583,6 +612,7 @@
             vmem((WROWS, TOK), F32),
             vmem((TOK, wide), BF),
             vmem((TOK, wide), BF),
+            vmem((TOK, D), BF),
             vmem((2, KVH, 5 * UNIT, HD), BF),
             vmem((KVH, 5 * UNIT, HD), BF),
             vmem((KVH, 3, UNIT, HD), BF),
@@ -590,10 +620,10 @@
             vmem((UNIT, HD), F32),
             vmem((2, KVH, 4, UNIT, HD), BF),
             vmem((ROWS, 2 * HD), F32),
-            vmem((16, 80, HD), F32),
-            vmem((2, 16, 80, HD), BF),
-            vmem((2, 16, 80, HD), BF),
-            vmem((80, HD), F32),
+            vmem((16, 176, HD), F32),
+            vmem((16, 176, HD), BF),
+            vmem((16, 176, HD), BF),
+            vmem((176, HD), F32),
             vmem((HD, 256), F32),
             vmem((1, HD), F32),
             vmem((8, HD), F32),
@@ -612,6 +642,22 @@
         kv_weight, hidden[0], queries[0], grad_out[0], doc_ids[0].reshape(16, TOK),
         q_gain.reshape(1, HD), k_gain.reshape(1, HD),
     )
+    def cut(width):
+        return pl.BlockSpec((TOK, width), lambda i: (0, i))
+
+    def whole(shape):
+        return pl.BlockSpec(shape, lambda i: (0, 0))
+
+    specs = [cut(1024), cut(1024), cut(D // 4), whole((20, 1024)), whole((1, HD)), whole((1, HD))]
+    results = (att, dq, gh, gw, qgo, kgo)
+    att, dq, gh, gw, qgo, kgo = pl.pallas_call(
+        finish_kernel,
+        grid=(4,),
+        out_shape=tuple(sds(r.shape, r.dtype) for r in results),
+        in_specs=specs,
+        out_specs=tuple(specs),
+        name="finish",
+    )(*results)
     return (att[None], dq[None], gh[None], gw, qgo.reshape(HD), kgo.reshape(HD))
 
 

time: 109 us -> 98.9 us (0.907)
  local copies, waits for them, and re-layouts: 6.48 us -> 0 us
  Pallas kernels: 101 us -> 97.9 us
    unnamed x16 -> x0, local copies, waits for them, and re-layouts: 6.48 us -> none
    pallas_call x1 -> x2, Pallas kernels: 101 us -> 97.9 us  [the longest x1 93.8 us: shards(): pl.pallas_call(mega_kernel, out_shape=(sds((TOK, wide), BF), sds((TOK, wi...]
where the time goes in v3:
time: 98.9 us; the launch traced here: 98.7 us
  Pallas kernels  97.9 us (99%)
    pallas_call x1, Pallas kernels, shards(): pl.pallas_call(mega_kernel, out_shape=(sds((TOK, wide), BF), sds((TOK, wi...  93.8 us
    pallas_call x1, Pallas kernels, shards(): pl.pallas_call(finish_kernel, grid=(4,), out_shape=tuple((sds(r.shape, r....  4.04 us

profile of v3, /device:TPU:1, one launch (start us, length us, event | category | flops | bytes accessed | tf_op | source)
XLA Modules:
  0.0 98.7 jit_solution(11002849416791460780)
XLA Ops:
  0.6 93.8 %mega.1 = (bf16[128,4096]{1,0:T(8,128)(2,1)}, bf16[128,4096]{1,0:T(8,128)(2,1)}, bf16[128,2560]{1,0:T(8,128)(2,1)}, bf16[20,1024]{1,0:T(8,128)(2,1)}, f32[1,128]{1,0:T(1,128)}, /*index=5*/f32[1,128]{1,0:T(1,128)}) custom-call(bf16[320,1024]{1,0:T(8,128)(2,1)} %w.1, bf16[128,2560]{1,0:T(8,128)(2,1)} %bitcast.13, bf16[128,4096]{1,0:T(8,128)(2,1)} %bitcast.11, ...), custom_call_target="tpu_custom_call" | custom-call | tf_op jit(solution)/shard_map/mega/pallas_call | solution.py:583
  94.5 4.0 %finish.1 = (bf16[128,4096]{1,0:T(8,128)(2,1)}, bf16[128,4096]{1,0:T(8,128)(2,1)}, bf16[128,2560]{1,0:T(8,128)(2,1)}, bf16[20,1024]{1,0:T(8,128)(2,1)}, f32[1,128]{1,0:T(1,128)}, /*index=5*/f32[1,128]{1,0:T(1,128)}) custom-call(bf16[128,4096]{1,0:T(8,128)(2,1)} %get-tuple-element.18.refs_0_, bf16[128,4096]{1,0:T(8,128)(2,1)} %get-tuple-element.19.refs_1_, ...), custom_call_target="tpu_custom_call" | custom-call | tf_op jit(solution)/shard_map/finish/pallas_call | solution.py:653

commit v4 on v3

--- a/solution.py
+++ b/solution.py
@@ -51,29 +51,39 @@
 
 
 class Net:
-    def __init__(self, send, recv):
-        self.send, self.recv, self.n = send, recv, 0
-        self.sent = []
-
-    def copy(self, src, dst, dev):
-        i = self.n
-        self.n += 1
+    def __init__(self, send, recv, dev):
+        self.send, self.recv, self.dev = send, recv, dev
+        self.sends, self.recvs, self.drains = 0, 0, []
+
+    def outgoing(self, whole, cond=None):
+        sem = self.send.at[self.sends]
+        self.sends += 1
+        self.drains.append((sem, whole, cond))
+        return sem
+
+    def incoming(self):
+        self.recvs += 1
+        return self.recv.at[self.recvs - 1]
+
+    def copy(self, src, dst, dev, out, into):
         return pltpu.make_async_remote_copy(
             src_ref=src,
             dst_ref=dst,
-            send_sem=self.send.at[i],
-            recv_sem=self.recv.at[i],
+            send_sem=out,
+            recv_sem=into,
             device_id=dev,
             device_id_type=MESH,
         )
 
-    def start(self, copy, cond=None):
-        self.sent.append((copy, cond))
-        when(cond, copy.start)
+    def go(self, src, dst, dev, out, into, cond=None):
+        when(cond, self.copy(src, dst, dev, out, into).start)
+
+    def arrived(self, whole, into, cond=None):
+        when(cond, self.copy(whole, whole, self.dev, self.send.at[0], into).wait_recv)
 
     def drain(self):
-        for copy, cond in self.sent:
-            when(cond, copy.wait_send)
+        for sem, whole, cond in self.drains:
+            when(cond, self.copy(whole, whole, self.dev, sem, self.recv.at[0]).wait_send)
 
 
 def when(cond, fn):
@@ -94,7 +104,8 @@
     return ((i // 8) * 8 + ((i // 2) % 4) * 2 + c) * 160 + ((i % 2) * 4 + z) * 20
 
 
-NSEM = 208
+NSEND = 24
+NRECV = 80
 WROWS = WIN * TOK
 UNIT = 2 * TOK
 CUTS = (pl.ds(0, 128), pl.ds(128, 48))
@@ -102,14 +113,15 @@
 
 
 def mega_kernel(
-    w, hid, q, do, docs, qg, kg,
-    att, dq, gh, gw, qgo, kgo,
+    w, hid, q, do, docs_in, qg_in, kg_in,
+    att, dq, gh, gw_out, qgo, kgo,
+    docs, qg, kg, gw, gsum,
     wbuf, hidv, hT, hpk, hb, kv, kraw, qv, dov, xh, rq, doT, qn, dos, w_s, ds_s, mask,
     attv, dqv, ghv, part, sb, xr, yr, t0, gb, gf, st, rbs, rbr, stf, gacc, kacc, gs1, gr1, gs2, gr2,
     send, recv, loc,
 ):
     p = Place()
-    net = Net(send, recv)
+    net = Net(send, recv, p.at(c=1 - p.c))
     c, x, z, k = p.c, p.x, p.z, p.k
     row1 = p.yl == 1
     sib = p.at(c=1 - c)
@@ -136,6 +148,8 @@
     loads.append(pltpu.make_async_copy(hid, hidv.at[c], loc.at[8]))
     loads.append(pltpu.make_async_copy(q, qv, loc.at[9]))
     loads.append(pltpu.make_async_copy(do, dov, loc.at[10]))
+    for n, (a, b) in enumerate(((docs_in, docs), (qg_in, qg), (kg_in, kg))):
+        loads.append(pltpu.make_async_copy(a, b, loc.at[12 + n]))
     for l in loads:
         l.start()
     for m in range(1, 5):
@@ -146,42 +160,48 @@
     for l in loads[:4]:
         l.wait()
 
-    def wcopy(f, j, lo, n, dev):
-        ref = wbuf.at[f, j, pl.ds(lo, n)]
-        cp = net.copy(ref, ref, dev)
-        net.start(cp)
-        return cp
-
     half, fourth = ROWS // 2, ROWS // 4
     mine4 = pl.multiple_of(x * fourth, 16)
-    quarter, zp0, zp1, zm0, zm1, far_c, zpf, zmf, xs_c = ([None] * KVH for _ in range(9))
+    w_out = net.outgoing(wbuf.at[pl.ds(0, 7), pl.ds(0, 4)])
+    in_zp, in_zm, in_quarter, in_direct, in_relayed = (
+        [net.incoming() for _ in range(KVH)] for _ in range(5)
+    )
+
+    def wcopy(f, j, lo, n, dev, into):
+        ref = wbuf.at[f, j, pl.ds(lo, n)]
+        net.go(ref, ref, dev, w_out, into)
 
     def push(g):
         j = cj + g
-        quarter[g] = [None] + [wcopy(p.f, j, mine4, fourth, fard[d]) for d in (1, 2, 3)]
-        zp0[g] = wcopy(p.f, j, 0, half, zd[1])
-        zm1[g] = wcopy(p.f, j, half, half, zd[3])
-        far_c[g] = wcopy(p.f, j, 0, ROWS, far)
-        zp1[g] = wcopy(p.f, j, half, half, zd[1])
-        zm0[g] = wcopy(p.f, j, 0, half, zd[3])
+        for d in (1, 2, 3):
+            wcopy(p.f, j, mine4, fourth, fard[d], in_quarter[g])
+        wcopy(p.f, j, 0, half, zd[1], in_zp[g])
+        wcopy(p.f, j, half, half, zd[3], in_zm[g])
+        wcopy(p.f, j, 0, ROWS, far, in_direct[g])
+        wcopy(p.f, j, half, half, zd[1], in_direct[g])
+        wcopy(p.f, j, 0, half, zd[3], in_direct[g])
+
+    def count(rows):
+        return part.at[0, 0, pl.ds(0, rows)]
 
     def relay(g):
         j = cj + g
-        zp0[g].wait_recv()
-        zpf[g] = wcopy(home + p.zs(3), j, 0, half, zd[1])
-        zm1[g].wait_recv()
-        zmf[g] = wcopy(home + p.zs(1), j, half, half, zd[3])
-        xs_c[g] = []
+        net.arrived(count(half), in_zp[g])
+        wcopy(home + p.zs(3), j, 0, half, zd[1], in_relayed[g])
+        net.arrived(count(half), in_zm[g])
+        wcopy(home + p.zs(1), j, half, half, zd[3], in_relayed[g])
+        net.arrived(count(3 * fourth), in_quarter[g])
         for d in (1, 3, 2):
-            quarter[g][d].wait_recv()
             for e in (1, 3, 2):
-                xs_c[g].append(wcopy(away + p.zs(4 - d), j, mine4, fourth, xd[e]))
+                wcopy(away + p.zs(4 - d), j, mine4, fourth, xd[e], in_relayed[g])
 
     push(0)
     loads[8].wait()
-    hs_c = net.copy(hidv.at[c], hidv.at[c], sib)
-    net.start(hs_c)
+    hs_in = net.incoming()
+    net.go(hidv.at[c], hidv.at[c], sib, net.outgoing(hidv.at[c]), hs_in)
     push(1)
+    for l in loads[4:8] + loads[11:]:
+        l.wait()
 
     gain = jnp.broadcast_to(qg[...], (HD, HD)).T
 
@@ -229,7 +249,7 @@
                 part[t, g, pl.ds(pl.multiple_of((1 - c) * WROWS, TOK), TOK), :] = jnp.zeros((TOK, HD), BF)
 
     mine = z * 2 + c
-    h_cps = []
+    h_in = net.incoming()
     own_h = pltpu.make_async_copy(hpk.at[mine], hb.at[mine], loc.at[11])
 
     def exchange_hidden():
@@ -239,10 +259,9 @@
             for cc in range(2):
                 for i in range(16):
                     hpk[zc * 2 + cc, pl.ds(i * 20, 20), :] = hT[pl.ds(piece_start(i, cc, zc), 20), :].astype(BF)
+        out = net.outgoing(hpk.at[pl.ds(0, 7)])
         for zc, cc in zgroup:
-            cp = net.copy(hpk.at[zc * 2 + cc], hb.at[mine], p.at(z=zc, c=cc))
-            net.start(cp)
-            h_cps.append(cp)
+            net.go(hpk.at[zc * 2 + cc], hb.at[mine], p.at(z=zc, c=cc), out, h_in)
         own_h.start()
 
     home_rows = pl.ds(4 * UNIT, UNIT)
@@ -250,13 +269,24 @@
     def unit(m):
         return pl.ds((4 - m) * UNIT, UNIT)
 
-    y_c, x_c, b_c = [], [], []
+    four = kv.at[c, :, pl.ds(0, UNIT)]
+    one = kv.at[c, 0, pl.ds(0, UNIT)]
+    y_out = net.outgoing(four, p.yl == 0)
+    x_out = [None] + [net.outgoing(four, row1 | (x + m <= 3)) for m in (1, 2, 3)]
+    b_out = net.outgoing(kv.at[c])
+    y_in = [net.incoming() for _ in range(KVH)]
+    x_in = [[None] + [net.incoming() for _ in range(3)] for _ in range(KVH)]
+    b_in = [net.incoming() for _ in range(KVH)]
+
+    def along_x(g, m, src, cond):
+        net.go(kv.at[c, g, src], kv.at[c, g, unit(m)], xd[m], x_out[m], x_in[g][m], cond)
+
 
     def project(g):
         if g == 0:
-            hs_c.wait_recv()
-        for cp in (zp1[g], zm0[g], far_c[g], zpf[g], zmf[g], *xs_c[g]):
-            cp.wait_recv()
+            net.arrived(hidv.at[c], hs_in)
+        net.arrived(count(2 * ROWS), in_direct[g])
+        net.arrived(count(ROWS + 9 * fourth), in_relayed[g])
         lhs = jnp.concatenate([hidv[0], hidv[1]], axis=0)
         raw = jnp.dot(lhs, wbuf[:, cj + g].reshape(D, 128), preferred_element_type=F32)
 
@@ -270,33 +300,24 @@
         def _():
             kv[1, g, home_rows, :] = raw.astype(BF)
 
-        cp = net.copy(kv.at[c, g, unit(0)], kv.at[c, g, unit(4)], near)
-        net.start(cp, p.yl == 0)
-        y_c.append(cp)
-        row = [None]
+        net.go(kv.at[c, g, unit(0)], kv.at[c, g, unit(4)], near, y_out, y_in[g], p.yl == 0)
         for m in (1, 2, 3):
-            src = kv.at[c, g, pl.ds(pl.multiple_of(jnp.where(x + m <= 3, 4 * UNIT, 0), UNIT), UNIT)]
-            cp = net.copy(src, kv.at[c, g, unit(m)], xd[m])
-            net.start(cp, x + m <= 3)
-            row.append(cp)
-        x_c.append(row)
+            along_x(g, m, unit(0), x + m <= 3)
 
     def spread(g):
-        when(row1, y_c[g].wait_recv)
+        net.arrived(one, y_in[g], row1)
         for m in (1, 2, 3):
-            net.start(x_c[g][m], row1 & (x + m > 3))
+            along_x(g, m, unit(4), row1 & (x + m > 3))
 
     def share(g):
         for m in (1, 2, 3):
-            when(k >= m, x_c[g][m].wait_recv)
-        cp = net.copy(kv.at[c, g], kv.at[c, g], sib)
-        net.start(cp)
-        b_c.append(cp)
+            net.arrived(one, x_in[g][m], k >= m)
+        net.go(kv.at[c, g], kv.at[c, g], sib, b_out, b_in[g])
 
     span = pl.ds(pl.multiple_of(c * TOK, TOK), WROWS)
 
     def open_head(g):
-        b_c[g].wait_recv()
+        net.arrived(kv.at[c, g], b_in[g])
         ka = kv[0, g, span, :]
         va = kv[1, g, span, :]
         return ka, va, ka.astype(F32).T.astype(BF), va.astype(F32).T.astype(BF)
@@ -343,42 +364,42 @@
         part[0, g, span, :] = dkk.astype(BF)
         cols = pl.ds(g * 1024, 1024)
         for n, (a, b) in enumerate(((attv, att), (dqv, dq))):
-            cp = pltpu.make_async_copy(a.at[:, cols], b.at[:, cols], loc.at[12 + g * 2 + n])
+            cp = pltpu.make_async_copy(a.at[:, cols], b.at[:, cols], loc.at[g * 2 + n])
             cp.start()
             outs.append(cp)
 
-    s_c, u_c, v_c, z_c, w_c = {}, {}, {}, {}, {}
+    s_out, w_out2 = net.outgoing(part.at[1 - c]), net.outgoing(gb.at[c])
+    u_out = [None] + [net.outgoing(four, k >= m) for m in (1, 2, 3)]
+    v_out = net.outgoing(four, row1)
+    z_out = net.outgoing(gb.at[c, :, pl.ds(0, 3)])
+    s_in, v_in, z_in, w_in = ([net.incoming() for _ in range(KVH)] for _ in range(4))
+    u_in = [[None] + [net.incoming() for _ in range(3)] for _ in range(KVH)]
 
     def c1(g):
-        s_c[g] = net.copy(part.at[1 - c, g], sb.at[g], sib)
-        net.start(s_c[g])
+        net.go(part.at[1 - c, g], sb.at[g], sib, s_out, s_in[g])
 
     def c2(g):
-        s_c[g].wait_recv()
+        net.arrived(sb.at[g], s_in[g])
         part[c, g] = (part[c, g].astype(F32) + sb[g].astype(F32)).astype(BF)
-        u_c[g] = [None]
         for m in (1, 2, 3):
-            cp = net.copy(part.at[c, g, unit(m)], xr.at[g, m - 1], xd[4 - m])
-            net.start(cp, k >= m)
-            u_c[g].append(cp)
+            net.go(part.at[c, g, unit(m)], xr.at[g, m - 1], xd[4 - m], u_out[m], u_in[g][m], k >= m)
 
     def c3(g):
         t0[...] = part[c, g, unit(0), :].astype(F32)
         for m in (1, 2, 3):
             @pl.when(x + m <= 3)
             def _():
-                u_c[g][m].wait_recv()
+                net.arrived(xr.at[g, m - 1], u_in[g][m])
                 t0[...] += xr[g, m - 1].astype(F32)
 
             @pl.when((x + m > 3) & row1)
             def _():
-                u_c[g][m].wait_recv()
+                net.arrived(xr.at[g, m - 1], u_in[g][m])
                 part[c, g, unit(4), :] = (
                     part[c, g, unit(4), :].astype(F32) + xr[g, m - 1].astype(F32)
                 ).astype(BF)
 
-        v_c[g] = net.copy(part.at[c, g, unit(4)], yr.at[g], near)
-        net.start(v_c[g], row1)
+        net.go(part.at[c, g, unit(4)], yr.at[g], near, v_out, v_in[g], row1)
         part[c, g, unit(0), :] = t0[...].astype(BF)
 
     def c4(g):
@@ -386,7 +407,7 @@
 
         @pl.when(p.yl == 0)
         def _():
-            v_c[g].wait_recv()
+            net.arrived(yr.at[g], v_in[g])
             t0[...] += yr[g].astype(F32)
 
         @pl.when(c == 0)
@@ -404,23 +425,18 @@
         def _():
             gb[1, g, z] = t0[...].astype(BF)
 
-        z_c[g] = []
         for d in (1, 3, 2):
-            cp = net.copy(gb.at[c, g, z], gb.at[c, g, z], zd[d])
-            net.start(cp)
-            z_c[g].append(cp)
+            net.go(gb.at[c, g, z], gb.at[c, g, z], zd[d], z_out, z_in[g])
 
     def d1(g):
-        for cp in z_c[g]:
-            cp.wait_recv()
-        w_c[g] = net.copy(gb.at[c, g], gb.at[c, g], sib)
-        net.start(w_c[g])
+        net.arrived(gb.at[c, g, pl.ds(0, 3)], z_in[g])
+        net.go(gb.at[c, g], gb.at[c, g], sib, w_out2, w_in[g])
 
     def offset(g, t):
         return (g * 2 + t) * 20 + (8 if g == 3 else 0)
 
     def weight_terms(g):
-        w_c[g].wait_recv()
+        net.arrived(gb.at[c, g], w_in[g])
         lhs = jnp.concatenate([hb[i] for i in range(8)], axis=1)
         rhs = jnp.concatenate([gb[0, g].reshape(8 * TOK, HD), gb[1, g].reshape(8 * TOK, HD)], axis=1)
         gf[...] = jnp.dot(lhs, rhs, preferred_element_type=F32)
@@ -428,24 +444,20 @@
             for t in range(2):
                 st[i, pl.ds(offset(g, t), 20), :] = gf[pl.ds(i * 20, 20), t * HD:(t + 1) * HD]
 
-    r_c = []
+    r_in = [net.incoming() for _ in CUTS]
 
     def scatter(n):
         rows = CUTS[n]
         for i in range(16):
             rbs[i, rows] = st[i, rows].astype(BF)
-        row = []
+        out = net.outgoing(rbs.at[pl.ds(0, 15), rows])
         for o, dev in peers:
-            cp = net.copy(rbs.at[o, rows], rbr.at[me16, rows], dev)
-            net.start(cp)
-            row.append(cp)
-        r_c.append(row)
+            net.go(rbs.at[o, rows], rbr.at[me16, rows], dev, out, r_in[n])
         rbr[me16, rows] = rbs[me16, rows]
 
     def collect(n):
         rows = CUTS[n]
-        for cp in r_c[n]:
-            cp.wait_recv()
+        net.arrived(rbr.at[pl.ds(0, 15), rows], r_in[n])
         total = rbr[0, rows].astype(F32)
         for i in range(1, 16):
             total = total + rbr[i, rows].astype(F32)
@@ -455,14 +467,13 @@
                 at = (t * 4 + g) * HD
                 gw[:, at:at + HD] = stf[pl.ds(offset(g, t), 20), :].astype(BF)
 
-    w_sib = []
+    w_in_sib = net.incoming()
 
     def weight_share():
+        out = net.outgoing(wbuf.at[pl.ds(0, 7), pl.ds(0, 4)])
         for f in (home + p.zs(1), home + p.zs(2), home + p.zs(3), away, away + 1, away + 2, away + 3):
             ref = wbuf.at[f, own]
-            cp = net.copy(ref, ref, sib)
-            net.start(cp)
-            w_sib.append(cp)
+            net.go(ref, ref, sib, out, w_in_sib)
 
     project(0)
     relay(2)
@@ -488,9 +499,10 @@
         6: [lambda: c2(0)],
         7: [lambda: c1(1)],
         10: [lambda: c2(1)],
-        11: [lambda: c3(0), lambda: c1(2)],
+        11: [lambda: c1(2)],
+        12: [lambda: c3(0)],
         14: [lambda: c2(2)],
-        15: [lambda: c1(3), lambda: c4(0)],
+        15: [lambda: c1(3)],
     }
     for g in range(KVH):
         head = open_head(g)
@@ -501,50 +513,43 @@
             for fn in todo.get(g * 4 + pair, ()):
                 fn()
 
+    c4(0)
     c3(1)
+    net.arrived(hpk.at[pl.ds(0, 7)], h_in)
+    own_h.wait()
     c2(3)
-    for cp in h_cps:
-        cp.wait_recv()
-    own_h.wait()
-    d1(0)
     c3(2)
     c4(1)
+    d1(0)
+    c3(3)
+    c4(2)
     weight_terms(0)
-    c3(3)
     d1(1)
-    c4(2)
-    weight_terms(1)
     c4(3)
     a = gacc[:, :HD] + gacc[:, HD:]
     gs1[...] = jnp.concatenate(
         [jnp.sum(a.T, axis=0, keepdims=True), kacc[...], jnp.zeros((6, HD), F32)], axis=0
     )
-    g1 = []
+    g1_in, g2_in = net.incoming(), net.incoming()
+    out = net.outgoing(gr1.at[pl.ds(0, 7)])
     for zc, cc in zgroup:
-        cp = net.copy(gs1, gr1.at[mine], p.at(z=zc, c=cc))
-        net.start(cp)
-        g1.append(cp)
+        net.go(gs1, gr1.at[mine], p.at(z=zc, c=cc), out, g1_in)
     gr1[mine] = gs1[...]
+    weight_terms(1)
     d1(2)
+    d1(3)
     weight_terms(2)
     scatter(0)
-    d1(3)
-    for cp in g1:
-        cp.wait_recv()
+    net.arrived(gr1.at[pl.ds(0, 7)], g1_in)
     gs2[...] = jnp.sum(gr1[...], axis=0)
-    g2 = []
+    out = net.outgoing(gr2.at[pl.ds(0, 15)])
     for o, dev in peers:
-        cp = net.copy(gs2, gr2.at[me16], dev)
-        net.start(cp)
-        g2.append(cp)
+        net.go(gs2, gr2.at[me16], dev, out, g2_in)
     gr2[me16] = gs2[...]
     weight_terms(3)
     scatter(1)
 
-    for l in loads[4:8]:
-        l.wait()
-    for cp in w_sib:
-        cp.wait_recv()
+    net.arrived(wbuf.at[pl.ds(0, 7), pl.ds(0, 4)], w_in_sib)
     tokens = pl.ds(pl.multiple_of(c * TOK, TOK), TOK)
     gkv = jnp.concatenate([gb[t, g, z, tokens, :] for t in range(2) for g in range(KVH)], axis=1)
     for f in range(8):
@@ -552,30 +557,48 @@
         ghv[:, f * ROWS:(f + 1) * ROWS] = lax.dot_general(
             gkv, wv, NT, preferred_element_type=F32
         ).astype(BF)
-    cp = pltpu.make_async_copy(ghv, gh, loc.at[4])
+    cp = pltpu.make_async_copy(ghv, gh, loc.at[8])
     cp.start()
     outs.append(cp)
     collect(0)
-    for cp in g2:
-        cp.wait_recv()
-    gsum = jnp.sum(gr2[...], axis=0)
-    qgo[...] = gsum[0:1]
-    kgo[...] = gsum[1:2]
+    net.arrived(gr2.at[pl.ds(0, 15)], g2_in)
+    gsum[...] = jnp.sum(gr2[...], axis=0)
+    collect(1)
+    for n, (a, b) in enumerate(((gw, gw_out), (gsum.at[pl.ds(0, 1)], qgo), (gsum.at[pl.ds(1, 1)], kgo))):
+        cp = pltpu.make_async_copy(a, b, loc.at[9 + n])
+        cp.start()
+        outs.append(cp)
+    net.drain()
     for cp in outs:
         cp.wait()
-    collect(1)
-    net.drain()
-    assert net.n <= NSEM
+    assert net.sends <= NSEND and net.recvs <= NRECV
 
 
 def finish_kernel(*refs):
-    n = len(refs) // 2
-    for a, b in zip(refs[:n], refs[n:]):
-        b[...] = a[...]
+    n = (len(refs) - 2) // 3
+    ins, outs, held = refs[:n], refs[n:2 * n], refs[2 * n:3 * n]
+    sem_in, sem_out = refs[3 * n:]
+    jobs = []
+    for a, b, h in zip(ins, outs, held):
+        parts = 4 if a.shape[0] == TOK else 1
+        width = a.shape[1] // parts
+        for i in range(parts):
+            at = (slice(None), pl.ds(i * width, width))
+            j = len(jobs)
+            jobs.append((
+                pltpu.make_async_copy(a.at[at], h.at[at], sem_in.at[j]),
+                pltpu.make_async_copy(h.at[at], b.at[at], sem_out.at[j]),
+            ))
+    for load, _ in jobs:
+        load.start()
+    for load, store in jobs:
+        load.wait()
+        store.start()
+    for _, store in jobs:
+        store.wait()
 
 
 def shards(hidden, queries, doc_ids, kv_weight, q_gain, k_gain, grad_out):
-    vm = pl.BlockSpec(memory_space=pltpu.VMEM)
     hbm = pl.BlockSpec(memory_space=pl.ANY)
     sds = jax.ShapeDtypeStruct
     vmem = pltpu.VMEM
@@ -590,9 +613,14 @@
             sds((1, HD), F32),
             sds((1, HD), F32),
         ),
-        in_specs=[hbm, hbm, hbm, hbm, vm, vm, vm],
-        out_specs=(hbm, hbm, hbm, vm, vm, vm),
+        in_specs=[hbm] * 7,
+        out_specs=(hbm,) * 6,
         scratch_shapes=[
+            vmem((16, TOK), jnp.int32),
+            vmem((1, HD), F32),
+            vmem((1, HD), F32),
+            vmem((20, 1024), BF),
+            vmem((8, HD), F32),
             vmem((8, 8, ROWS, 128), BF),
             vmem((2, TOK, D), BF),
             vmem((D, TOK), F32),
@@ -630,9 +658,9 @@
             vmem((8, 8, HD), F32),
             vmem((8, HD), F32),
             vmem((16, 8, HD), F32),
-            pltpu.SemaphoreType.DMA((NSEM,)),
-            pltpu.SemaphoreType.DMA((NSEM,)),
-            pltpu.SemaphoreType.DMA((20,)),
+            pltpu.SemaphoreType.DMA((NSEND,)),
+            pltpu.SemaphoreType.DMA((NRECV,)),
+            pltpu.SemaphoreType.DMA((15,)),
         ],
         compiler_params=pltpu.CompilerParams(
             collective_id=0, has_side_effects=True, vmem_limit_bytes=60 * 1024 * 1024
@@ -642,20 +670,15 @@
         kv_weight, hidden[0], queries[0], grad_out[0], doc_ids[0].reshape(16, TOK),
         q_gain.reshape(1, HD), k_gain.reshape(1, HD),
     )
-    def cut(width):
-        return pl.BlockSpec((TOK, width), lambda i: (0, i))
-
-    def whole(shape):
-        return pl.BlockSpec(shape, lambda i: (0, 0))
-
-    specs = [cut(1024), cut(1024), cut(D // 4), whole((20, 1024)), whole((1, HD)), whole((1, HD))]
     results = (att, dq, gh, gw, qgo, kgo)
     att, dq, gh, gw, qgo, kgo = pl.pallas_call(
         finish_kernel,
-        grid=(4,),
         out_shape=tuple(sds(r.shape, r.dtype) for r in results),
-        in_specs=specs,
-        out_specs=tuple(specs),
+        in_specs=[hbm] * 6,
+        out_specs=(hbm,) * 6,
+        scratch_shapes=[vmem(r.shape, r.dtype) for r in results]
+        + [pltpu.SemaphoreType.DMA((15,))] * 2,
+        compiler_params=pltpu.CompilerParams(vmem_limit_bytes=16 * 1024 * 1024),
         name="finish",
     )(*results)
     return (att[None], dq[None], gh[None], gw, qgo.reshape(HD), kgo.reshape(HD))

time: 98.9 us -> 98.4 us (level); the launches traced: 98.7 us -> 96.6 us
  Pallas kernels: 97.9 us -> 90.8 us
  local copies, waits for them, and re-layouts: 0 us -> 4.94 us
    pallas_call x1, Pallas kernels: 93.8 us -> 88.8 us  [shards(): pl.pallas_call(mega_kernel, out_shape=(sds((TOK, wide), BF), sds((TOK, wi...]
    unnamed x0 -> x12, local copies, waits for them, and re-layouts: none -> 4.94 us
    pallas_call x1, Pallas kernels: 4.04 us -> 2.07 us  [shards(): pl.pallas_call(finish_kernel, out_shape=tuple((sds(r.shape, r.dtype) for...]
where the time goes in v4:
time: 98.4 us; the launch traced here: 96.6 us
  Pallas kernels  90.8 us (92%)
  local copies, waits for them, and re-layouts  4.94 us (5%)
    pallas_call x1, Pallas kernels, shards(): pl.pallas_call(mega_kernel, out_shape=(sds((TOK, wide), BF), sds((TOK, wi...  88.8 us
    unnamed x12, local copies, waits for them, and re-layouts  4.94 us
    pallas_call x1, Pallas kernels, shards(): pl.pallas_call(finish_kernel, out_shape=tuple((sds(r.shape, r.dtype) for...  2.07 us

profile of v4, /device:TPU:1, one launch (start us, length us, event | category | flops | bytes accessed | tf_op | source)
XLA Modules:
  0.0 96.6 jit_solution(7732178440696743269)
XLA Ops:
  0.6 88.8 %mega.1 = (bf16[128,4096]{1,0:T(8,128)(2,1)}, bf16[128,4096]{1,0:T(8,128)(2,1)}, bf16[128,2560]{1,0:T(8,128)(2,1)}, bf16[20,1024]{1,0:T(8,128)(2,1)}, f32[1,128]{1,0:T(1,128)}, /*index=5*/f32[1,128]{1,0:T(1,128)}) custom-call(bf16[320,1024]{1,0:T(8,128)(2,1)} %w.1, bf16[128,2560]{1,0:T(8,128)(2,1)} %bitcast.13, bf16[128,4096]{1,0:T(8,128)(2,1)} %bitcast.11, ...), custom_call_target="tpu_custom_call" | custom-call | tf_op jit(solution)/shard_map/mega/pallas_call | solution.py:606
  89.4 0.0 copy-start.4
  89.4 0.0 copy-start.5
  89.4 0.6 copy-done.4
  90.0 0.0 copy-done.5
  90.0 0.0 copy-start
  90.0 1.2 %copy-done = bf16[128,4096]{1,0:T(8,128)(2,1)S(1)} copy-done((bf16[128,4096]{1,0:T(8,128)(2,1)S(1)}, bf16[128,4096]{1,0:T(8,128)(2,1)}, u32[]{:S(2)}) %copy-start) | copy-done | bytes 1048600
  91.3 0.0 copy-start.1
  91.3 1.2 %copy-done.1 = bf16[128,4096]{1,0:T(8,128)(2,1)S(1)} copy-done((bf16[128,4096]{1,0:T(8,128)(2,1)S(1)}, bf16[128,4096]{1,0:T(8,128)(2,1)}, u32[]{:S(2)}) %copy-start.1) | copy-done | bytes 1048600
  92.5 0.0 copy-start.2
  92.5 1.1 %copy-done.2 = bf16[128,2560]{1,0:T(8,128)(2,1)S(1)} copy-done((bf16[128,2560]{1,0:T(8,128)(2,1)S(1)}, bf16[128,2560]{1,0:T(8,128)(2,1)}, u32[]{:S(2)}) %copy-start.2) | copy-done | bytes 655384
  93.6 0.0 copy-start.3
  93.6 0.8 copy-done.3
  94.4 2.1 %finish.1 = (bf16[128,4096]{1,0:T(8,128)(2,1)}, bf16[128,4096]{1,0:T(8,128)(2,1)}, bf16[128,2560]{1,0:T(8,128)(2,1)}, bf16[20,1024]{1,0:T(8,128)(2,1)}, f32[1,128]{1,0:T(1,128)}, /*index=5*/f32[1,128]{1,0:T(1,128)}) custom-call(bf16[128,4096]{1,0:T(8,128)(2,1)S(1)} %copy-done, bf16[128,4096]{1,0:T(8,128)(2,1)S(1)} %copy-done.1, ...), custom_call_target="tpu_custom_call" | custom-call | tf_op jit(solution)/shard_map/finish/pallas_call | solution.py:674
Async XLA Ops:
  89.4 0.6 copy-start.4
  89.4 0.6 copy-start.5
  90.0 1.2 %copy-start = (bf16[128,4096]{1,0:T(8,128)(2,1)S(1)}, bf16[128,4096]{1,0:T(8,128)(2,1)}, u32[]{:S(2)}) copy-start(bf16[128,4096]{1,0:T(8,128)(2,1)} %get-tuple-element.18.refs_0_) | copy-start | bytes 3145732
  91.3 1.2 %copy-start.1 = (bf16[128,4096]{1,0:T(8,128)(2,1)S(1)}, bf16[128,4096]{1,0:T(8,128)(2,1)}, u32[]{:S(2)}) copy-start(bf16[128,4096]{1,0:T(8,128)(2,1)} %get-tuple-element.19.refs_1_) | copy-start | bytes 3145732
  92.5 1.1 %copy-start.2 = (bf16[128,2560]{1,0:T(8,128)(2,1)S(1)}, bf16[128,2560]{1,0:T(8,128)(2,1)}, u32[]{:S(2)}) copy-start(bf16[128,2560]{1,0:T(8,128)(2,1)} %get-tuple-element.20.refs_2_) | copy-start | bytes 1966084
  93.6 0.8 copy-start.3

commit v5 on v4

--- a/solution.py
+++ b/solution.py
@@ -105,7 +105,7 @@
 
 
 NSEND = 24
-NRECV = 80
+NRECV = 88
 WROWS = WIN * TOK
 UNIT = 2 * TOK
 CUTS = (pl.ds(0, 128), pl.ds(128, 48))
@@ -372,8 +372,16 @@
     u_out = [None] + [net.outgoing(four, k >= m) for m in (1, 2, 3)]
     v_out = net.outgoing(four, row1)
     z_out = net.outgoing(gb.at[c, :, pl.ds(0, 3)])
-    s_in, v_in, z_in, w_in = ([net.incoming() for _ in range(KVH)] for _ in range(4))
-    u_in = [[None] + [net.incoming() for _ in range(3)] for _ in range(KVH)]
+    s_in = [net.incoming() for _ in range(KVH)]
+    pieces = [(g, h) for g in range(KVH) for h in ((None,) if g < KVH - 1 else (0, 1))]
+    v_in, z_in, w_in = ({key: net.incoming() for key in pieces} for _ in range(3))
+    u_in = {(g, h, m): net.incoming() for g, h in pieces for m in (1, 2, 3)}
+
+    def part_of(h, start=0):
+        return pl.ds(start, UNIT) if h is None else pl.ds(start + h * TOK, TOK)
+
+    def unit_of(m, h):
+        return part_of(h, (4 - m) * UNIT)
 
     def c1(g):
         net.go(part.at[1 - c, g], sb.at[g], sib, s_out, s_in[g])
@@ -381,62 +389,73 @@
     def c2(g):
         net.arrived(sb.at[g], s_in[g])
         part[c, g] = (part[c, g].astype(F32) + sb[g].astype(F32)).astype(BF)
-        for m in (1, 2, 3):
-            net.go(part.at[c, g, unit(m)], xr.at[g, m - 1], xd[4 - m], u_out[m], u_in[g][m], k >= m)
-
-    def c3(g):
-        t0[...] = part[c, g, unit(0), :].astype(F32)
+        for h in [h for gg, h in pieces if gg == g]:
+            for m in (1, 2, 3):
+                net.go(
+                    part.at[c, g, unit_of(m, h)], xr.at[g, m - 1, part_of(h)], xd[4 - m],
+                    u_out[m], u_in[g, h, m], k >= m,
+                )
+
+    def c3(g, h=None):
+        rows = part_of(h)
+        t0[rows] = part[c, g, unit_of(0, h), :].astype(F32)
         for m in (1, 2, 3):
             @pl.when(x + m <= 3)
             def _():
-                net.arrived(xr.at[g, m - 1], u_in[g][m])
-                t0[...] += xr[g, m - 1].astype(F32)
+                net.arrived(xr.at[g, m - 1, rows], u_in[g, h, m])
+                t0[rows] += xr[g, m - 1, rows].astype(F32)
 
             @pl.when((x + m > 3) & row1)
             def _():
-                net.arrived(xr.at[g, m - 1], u_in[g][m])
-                part[c, g, unit(4), :] = (
-                    part[c, g, unit(4), :].astype(F32) + xr[g, m - 1].astype(F32)
+                net.arrived(xr.at[g, m - 1, rows], u_in[g, h, m])
+                part[c, g, unit_of(4, h), :] = (
+                    part[c, g, unit_of(4, h), :].astype(F32) + xr[g, m - 1, rows].astype(F32)
                 ).astype(BF)
 
-        net.go(part.at[c, g, unit(4)], yr.at[g], near, v_out, v_in[g], row1)
-        part[c, g, unit(0), :] = t0[...].astype(BF)
-
-    def c4(g):
-        t0[...] = part[c, g, unit(0), :].astype(F32)
+        net.go(part.at[c, g, unit_of(4, h)], yr.at[g, rows], near, v_out, v_in[g, h], row1)
+        part[c, g, unit_of(0, h), :] = t0[rows].astype(BF)
+
+    def c4(g, h=None):
+        rows = part_of(h)
+        t0[rows] = part[c, g, unit_of(0, h), :].astype(F32)
 
         @pl.when(p.yl == 0)
         def _():
-            net.arrived(yr.at[g], v_in[g])
-            t0[...] += yr[g].astype(F32)
+            net.arrived(yr.at[g, rows], v_in[g, h])
+            t0[rows] += yr[g, rows].astype(F32)
 
         @pl.when(c == 0)
         def _():
-            raw = kraw[g]
+            raw = kraw[g, rows]
             r = lax.rsqrt(jnp.mean(raw * raw, axis=1, keepdims=True) + EPS)
             xhat = raw * r
-            dy = t0[...]
+            dy = t0[rows]
             kacc[...] += jnp.sum(dy * xhat, axis=0, keepdims=True)
             dxh = dy * kg[...]
             dx = r * (dxh - xhat * jnp.mean(xhat * dxh, axis=1, keepdims=True))
-            gb[0, g, z] = dx.astype(BF)
+            gb[0, g, z, rows] = dx.astype(BF)
 
         @pl.when(c == 1)
         def _():
-            gb[1, g, z] = t0[...].astype(BF)
-
+            gb[1, g, z, rows] = t0[rows].astype(BF)
+
+        ref = gb.at[c, g, z, rows]
         for d in (1, 3, 2):
-            net.go(gb.at[c, g, z], gb.at[c, g, z], zd[d], z_out, z_in[g])
-
-    def d1(g):
-        net.arrived(gb.at[c, g, pl.ds(0, 3)], z_in[g])
-        net.go(gb.at[c, g], gb.at[c, g], sib, w_out2, w_in[g])
+            net.go(ref, ref, zd[d], z_out, z_in[g, h])
+
+    def d1(g, h=None):
+        rows = part_of(h)
+        net.arrived(gb.at[c, g, pl.ds(0, 3), rows], z_in[g, h])
+        ref = gb.at[c, g, :, rows]
+        net.go(ref, ref, sib, w_out2, w_in[g, h])
 
     def offset(g, t):
         return (g * 2 + t) * 20 + (8 if g == 3 else 0)
 
     def weight_terms(g):
-        net.arrived(gb.at[c, g], w_in[g])
+        for gg, h in pieces:
+            if gg == g:
+                net.arrived(gb.at[c, g, :, part_of(h)], w_in[g, h])
         lhs = jnp.concatenate([hb[i] for i in range(8)], axis=1)
         rhs = jnp.concatenate([gb[0, g].reshape(8 * TOK, HD), gb[1, g].reshape(8 * TOK, HD)], axis=1)
         gf[...] = jnp.dot(lhs, rhs, preferred_element_type=F32)
@@ -469,38 +488,40 @@
 
     w_in_sib = net.incoming()
 
-    def weight_share():
-        out = net.outgoing(wbuf.at[pl.ds(0, 7), pl.ds(0, 4)])
+    share_out = net.outgoing(wbuf.at[pl.ds(0, 7), pl.ds(0, 4)])
+
+    def weight_share(n):
         for f in (home + p.zs(1), home + p.zs(2), home + p.zs(3), away, away + 1, away + 2, away + 3):
-            ref = wbuf.at[f, own]
-            net.go(ref, ref, sib, out, w_in_sib)
+            ref = wbuf.at[f, cj + n]
+            net.go(ref, ref, sib, share_out, w_in_sib)
 
     project(0)
     relay(2)
+    prep(3)
     project(1)
-    prep(3)
+    spread(0)
     relay(3)
-    spread(0)
     window_mask()
     clear()
     project(2)
     spread(1)
+    share(0)
     exchange_hidden()
-    share(0)
     project(3)
     spread(2)
 
     todo = {
-        0: [lambda: share(1)],
-        1: [lambda: spread(3)],
-        2: [lambda: share(2), weight_share],
+        0: [lambda: share(1), lambda: spread(3)],
         3: [lambda: c1(0)],
-        5: [lambda: share(3)],
+        4: [lambda: share(2)],
+        5: [lambda: weight_share(0)],
         6: [lambda: c2(0)],
-        7: [lambda: c1(1)],
+        7: [lambda: c1(1), lambda: share(3)],
+        8: [lambda: weight_share(1)],
+        9: [lambda: weight_share(2)],
         10: [lambda: c2(1)],
         11: [lambda: c1(2)],
-        12: [lambda: c3(0)],
+        12: [lambda: c3(0), lambda: weight_share(3)],
         14: [lambda: c2(2)],
         15: [lambda: c1(3)],
     }
@@ -521,11 +542,13 @@
     c3(2)
     c4(1)
     d1(0)
-    c3(3)
+    c3(3, 0)
+    c3(3, 1)
     c4(2)
     weight_terms(0)
     d1(1)
-    c4(3)
+    c4(3, 0)
+    c4(3, 1)
     a = gacc[:, :HD] + gacc[:, HD:]
     gs1[...] = jnp.concatenate(
         [jnp.sum(a.T, axis=0, keepdims=True), kacc[...], jnp.zeros((6, HD), F32)], axis=0
@@ -537,7 +560,8 @@
     gr1[mine] = gs1[...]
     weight_terms(1)
     d1(2)
-    d1(3)
+    d1(3, 0)
+    d1(3, 1)
     weight_terms(2)
     scatter(0)
     net.arrived(gr1.at[pl.ds(0, 7)], g1_in)
@@ -678,7 +702,7 @@
         out_specs=(hbm,) * 6,
         scratch_shapes=[vmem(r.shape, r.dtype) for r in results]
         + [pltpu.SemaphoreType.DMA((15,))] * 2,
-        compiler_params=pltpu.CompilerParams(vmem_limit_bytes=16 * 1024 * 1024),
+        compiler_params=pltpu.CompilerParams(vmem_limit_bytes=60 * 1024 * 1024),
         name="finish",
     )(*results)
     return (att[None], dq[None], gh[None], gw, qgo.reshape(HD), kgo.reshape(HD))

time: 98.4 us -> 92.7 us (0.942); the launches traced: 96.6 us -> 92.5 us
  local copies, waits for them, and re-layouts: 4.94 us -> 0 us
    unnamed x12 -> x0, local copies, waits for them, and re-layouts: 4.94 us -> none
where the time goes in v5:
time: 92.7 us; the launch traced here: 92.5 us
  Pallas kernels  91.7 us (99%)
    pallas_call x1, Pallas kernels, shards(): pl.pallas_call(mega_kernel, out_shape=(sds((TOK, wide), BF), sds((TOK, wi...  89 us
    pallas_call x1, Pallas kernels, shards(): pl.pallas_call(finish_kernel, out_shape=tuple((sds(r.shape, r.dtype) for...  2.74 us

profile of v5, /device:TPU:1, one launch (start us, length us, event | category | flops | bytes accessed | tf_op | source)
XLA Modules:
  0.0 92.5 jit_solution(7473668992905016781)
XLA Ops:
  0.6 89.0 %mega.1 = (bf16[128,4096]{1,0:T(8,128)(2,1)}, bf16[128,4096]{1,0:T(8,128)(2,1)}, bf16[128,2560]{1,0:T(8,128)(2,1)}, bf16[20,1024]{1,0:T(8,128)(2,1)}, f32[1,128]{1,0:T(1,128)}, /*index=5*/f32[1,128]{1,0:T(1,128)}) custom-call(bf16[320,1024]{1,0:T(8,128)(2,1)} %w.1, bf16[128,2560]{1,0:T(8,128)(2,1)} %bitcast.13, bf16[128,4096]{1,0:T(8,128)(2,1)} %bitcast.11, ...), custom_call_target="tpu_custom_call" | custom-call | tf_op jit(solution)/shard_map/mega/pallas_call | solution.py:630
  89.6 2.7 %finish.1 = (bf16[128,4096]{1,0:T(8,128)(2,1)}, bf16[128,4096]{1,0:T(8,128)(2,1)}, bf16[128,2560]{1,0:T(8,128)(2,1)}, bf16[20,1024]{1,0:T(8,128)(2,1)}, f32[1,128]{1,0:T(1,128)}, /*index=5*/f32[1,128]{1,0:T(1,128)}) custom-call(bf16[128,4096]{1,0:T(8,128)(2,1)} %get-tuple-element.18.refs_0_, bf16[128,4096]{1,0:T(8,128)(2,1)} %get-tuple-element.19.refs_1_, ...), custom_call_target="tpu_custom_call" | custom-call | tf_op jit(solution)/shard_map/finish/pallas_call | solution.py:698

commit v6 on v5

--- a/solution.py
+++ b/solution.py
@@ -108,8 +108,7 @@
 NRECV = 88
 WROWS = WIN * TOK
 UNIT = 2 * TOK
-CUTS = (pl.ds(0, 128), pl.ds(128, 48))
-HEADS = ((0, 1, 2), (3,))
+CUTS = tuple(pl.ds(g * 48, 48) for g in range(KVH))
 
 
 def mega_kernel(
@@ -450,7 +449,7 @@
         net.go(ref, ref, sib, w_out2, w_in[g, h])
 
     def offset(g, t):
-        return (g * 2 + t) * 20 + (8 if g == 3 else 0)
+        return g * 48 + t * 20
 
     def weight_terms(g):
         for gg, h in pieces:
@@ -481,10 +480,9 @@
         for i in range(1, 16):
             total = total + rbr[i, rows].astype(F32)
         stf[rows] = total
-        for g in HEADS[n]:
-            for t in range(2):
-                at = (t * 4 + g) * HD
-                gw[:, at:at + HD] = stf[pl.ds(offset(g, t), 20), :].astype(BF)
+        for t in range(2):
+            at = (t * 4 + n) * HD
+            gw[:, at:at + HD] = stf[pl.ds(offset(n, t), 20), :].astype(BF)
 
     w_in_sib = net.incoming()
 
@@ -512,17 +510,11 @@
 
     todo = {
         0: [lambda: share(1), lambda: spread(3)],
-        3: [lambda: c1(0)],
-        4: [lambda: share(2)],
-        5: [lambda: weight_share(0)],
-        6: [lambda: c2(0)],
-        7: [lambda: c1(1), lambda: share(3)],
-        8: [lambda: weight_share(1)],
-        9: [lambda: weight_share(2)],
-        10: [lambda: c2(1)],
-        11: [lambda: c1(2)],
-        12: [lambda: c3(0), lambda: weight_share(3)],
-        14: [lambda: c2(2)],
+        3: [lambda: c1(0), lambda: share(2)],
+        7: [lambda: c2(0), lambda: share(3), lambda: c1(1), lambda: weight_share(0)],
+        10: [lambda: c2(1), lambda: weight_share(1)],
+        11: [lambda: c1(2), lambda: weight_share(2)],
+        14: [lambda: c3(0), lambda: c2(2), lambda: weight_share(3)],
         15: [lambda: c1(3)],
     }
     for g in range(KVH):
@@ -546,6 +538,7 @@
     c3(3, 1)
     c4(2)
     weight_terms(0)
+    scatter(0)
     d1(1)
     c4(3, 0)
     c4(3, 1)
@@ -559,11 +552,12 @@
         net.go(gs1, gr1.at[mine], p.at(z=zc, c=cc), out, g1_in)
     gr1[mine] = gs1[...]
     weight_terms(1)
+    scatter(1)
     d1(2)
     d1(3, 0)
     d1(3, 1)
     weight_terms(2)
-    scatter(0)
+    scatter(2)
     net.arrived(gr1.at[pl.ds(0, 7)], g1_in)
     gs2[...] = jnp.sum(gr1[...], axis=0)
     out = net.outgoing(gr2.at[pl.ds(0, 15)])
@@ -571,7 +565,7 @@
         net.go(gs2, gr2.at[me16], dev, out, g2_in)
     gr2[me16] = gs2[...]
     weight_terms(3)
-    scatter(1)
+    scatter(3)
 
     net.arrived(wbuf.at[pl.ds(0, 7), pl.ds(0, 4)], w_in_sib)
     tokens = pl.ds(pl.multiple_of(c * TOK, TOK), TOK)
@@ -585,9 +579,11 @@
     cp.start()
     outs.append(cp)
     collect(0)
+    collect(1)
+    collect(2)
     net.arrived(gr2.at[pl.ds(0, 15)], g2_in)
     gsum[...] = jnp.sum(gr2[...], axis=0)
-    collect(1)
+    collect(3)
     for n, (a, b) in enumerate(((gw, gw_out), (gsum.at[pl.ds(0, 1)], qgo), (gsum.at[pl.ds(1, 1)], kgo))):
         cp = pltpu.make_async_copy(a, b, loc.at[9 + n])
         cp.start()
@@ -672,10 +668,10 @@
             vmem((UNIT, HD), F32),
             vmem((2, KVH, 4, UNIT, HD), BF),
             vmem((ROWS, 2 * HD), F32),
-            vmem((16, 176, HD), F32),
-            vmem((16, 176, HD), BF),
-            vmem((16, 176, HD), BF),
-            vmem((176, HD), F32),
+            vmem((16, 192, HD), F32),
+            vmem((16, 192, HD), BF),
+            vmem((16, 192, HD), BF),
+            vmem((192, HD), F32),
             vmem((HD, 256), F32),
             vmem((1, HD), F32),
             vmem((8, HD), F32),

time: 92.7 us -> 87.6 us (0.945)
  Pallas kernels: 91.7 us -> 86.5 us
    pallas_call x1, Pallas kernels: 89 us -> 83.7 us  [shards(): pl.pallas_call(mega_kernel, out_shape=(sds((TOK, wide), BF), sds((TOK, wi...]
where the time goes in v6:
time: 87.6 us; the launch traced here: 87.3 us
  Pallas kernels  86.5 us (99%)
    pallas_call x1, Pallas kernels, shards(): pl.pallas_call(mega_kernel, out_shape=(sds((TOK, wide), BF), sds((TOK, wi...  83.7 us
    pallas_call x1, Pallas kernels, shards(): pl.pallas_call(finish_kernel, out_shape=tuple((sds(r.shape, r.dtype) for...  2.74 us

profile of v6, /device:TPU:1, one launch (start us, length us, event | category | flops | bytes accessed | tf_op | source)
XLA Modules:
  0.0 87.3 jit_solution(450245035270564170)
XLA Ops:
  0.6 83.7 %mega.1 = (bf16[128,4096]{1,0:T(8,128)(2,1)}, bf16[128,4096]{1,0:T(8,128)(2,1)}, bf16[128,2560]{1,0:T(8,128)(2,1)}, bf16[20,1024]{1,0:T(8,128)(2,1)}, f32[1,128]{1,0:T(1,128)}, /*index=5*/f32[1,128]{1,0:T(1,128)}) custom-call(bf16[320,1024]{1,0:T(8,128)(2,1)} %w.1, bf16[128,2560]{1,0:T(8,128)(2,1)} %bitcast.13, bf16[128,4096]{1,0:T(8,128)(2,1)} %bitcast.11, ...), custom_call_target="tpu_custom_call" | custom-call | tf_op jit(solution)/shard_map/mega/pallas_call | solution.py:626
  84.4 2.7 %finish.1 = (bf16[128,4096]{1,0:T(8,128)(2,1)}, bf16[128,4096]{1,0:T(8,128)(2,1)}, bf16[128,2560]{1,0:T(8,128)(2,1)}, bf16[20,1024]{1,0:T(8,128)(2,1)}, f32[1,128]{1,0:T(1,128)}, /*index=5*/f32[1,128]{1,0:T(1,128)}) custom-call(bf16[128,4096]{1,0:T(8,128)(2,1)} %get-tuple-element.18.refs_0_, bf16[128,4096]{1,0:T(8,128)(2,1)} %get-tuple-element.19.refs_1_, ...), custom_call_target="tpu_custom_call" | custom-call | tf_op jit(solution)/shard_map/finish/pallas_call | solution.py:694

commit v7 on v6

--- a/solution.py
+++ b/solution.py
@@ -506,16 +506,17 @@
     share(0)
     exchange_hidden()
     project(3)
-    spread(2)
 
     todo = {
-        0: [lambda: share(1), lambda: spread(3)],
+        0: [lambda: spread(2), lambda: share(1)],
+        1: [lambda: spread(3)],
         3: [lambda: c1(0), lambda: share(2)],
-        7: [lambda: c2(0), lambda: share(3), lambda: c1(1), lambda: weight_share(0)],
+        6: [lambda: c2(0)],
+        7: [lambda: share(3), lambda: c1(1), lambda: weight_share(0)],
         10: [lambda: c2(1), lambda: weight_share(1)],
-        11: [lambda: c1(2), lambda: weight_share(2)],
-        14: [lambda: c3(0), lambda: c2(2), lambda: weight_share(3)],
-        15: [lambda: c1(3)],
+        11: [lambda: c1(2), lambda: c3(0), lambda: weight_share(2)],
+        14: [lambda: c2(2), lambda: weight_share(3)],
+        15: [lambda: c1(3), lambda: c4(0)],
     }
     for g in range(KVH):
         head = open_head(g)
@@ -526,22 +527,21 @@
             for fn in todo.get(g * 4 + pair, ()):
                 fn()
 
-    c4(0)
     c3(1)
-    net.arrived(hpk.at[pl.ds(0, 7)], h_in)
-    own_h.wait()
     c2(3)
+    c4(1)
     c3(2)
-    c4(1)
-    d1(0)
     c3(3, 0)
     c3(3, 1)
     c4(2)
+    d1(0)
+    c4(3, 0)
+    c4(3, 1)
+    net.arrived(hpk.at[pl.ds(0, 7)], h_in)
+    own_h.wait()
+    d1(1)
     weight_terms(0)
     scatter(0)
-    d1(1)
-    c4(3, 0)
-    c4(3, 1)
     a = gacc[:, :HD] + gacc[:, HD:]
     gs1[...] = jnp.concatenate(
         [jnp.sum(a.T, axis=0, keepdims=True), kacc[...], jnp.zeros((6, HD), F32)], axis=0

time: 87.6 us -> 87.8 us (level)
  no operation moved by 1% of the time
where the time goes in v7:
time: 87.8 us; the launch traced here: 87.7 us
  Pallas kernels  86.8 us (99%)
    pallas_call x1, Pallas kernels, shards(): pl.pallas_call(mega_kernel, out_shape=(sds((TOK, wide), BF), sds((TOK, wi...  84.1 us
    pallas_call x1, Pallas kernels, shards(): pl.pallas_call(finish_kernel, out_shape=tuple((sds(r.shape, r.dtype) for...  2.74 us

profile of v7, /device:TPU:1, one launch (start us, length us, event | category | flops | bytes accessed | tf_op | source)
XLA Modules:
  0.0 87.7 jit_solution(12713366192723320509)
XLA Ops:
  0.6 84.1 %mega.1 = (bf16[128,4096]{1,0:T(8,128)(2,1)}, bf16[128,4096]{1,0:T(8,128)(2,1)}, bf16[128,2560]{1,0:T(8,128)(2,1)}, bf16[20,1024]{1,0:T(8,128)(2,1)}, f32[1,128]{1,0:T(1,128)}, /*index=5*/f32[1,128]{1,0:T(1,128)}) custom-call(bf16[320,1024]{1,0:T(8,128)(2,1)} %w.1, bf16[128,2560]{1,0:T(8,128)(2,1)} %bitcast.13, bf16[128,4096]{1,0:T(8,128)(2,1)} %bitcast.11, ...), custom_call_target="tpu_custom_call" | custom-call | tf_op jit(solution)/shard_map/mega/pallas_call | solution.py:626
  84.7 2.7 %finish.1 = (bf16[128,4096]{1,0:T(8,128)(2,1)}, bf16[128,4096]{1,0:T(8,128)(2,1)}, bf16[128,2560]{1,0:T(8,128)(2,1)}, bf16[20,1024]{1,0:T(8,128)(2,1)}, f32[1,128]{1,0:T(1,128)}, /*index=5*/f32[1,128]{1,0:T(1,128)}) custom-call(bf16[128,4096]{1,0:T(8,128)(2,1)} %get-tuple-element.18.refs_0_, bf16[128,4096]{1,0:T(8,128)(2,1)} %get-tuple-element.19.refs_1_, ...), custom_call_target="tpu_custom_call" | custom-call | tf_op jit(solution)/shard_map/finish/pallas_call | solution.py:694

commit v8 on v7

--- a/solution.py
+++ b/solution.py
@@ -107,6 +107,7 @@
 NSEND = 24
 NRECV = 88
 WROWS = WIN * TOK
+STEP = 4
 UNIT = 2 * TOK
 CUTS = tuple(pl.ds(g * 48, 48) for g in range(KVH))
 
@@ -321,16 +322,16 @@
         va = kv[1, g, span, :]
         return ka, va, ka.astype(F32).T.astype(BF), va.astype(F32).T.astype(BF)
 
-    gain2 = jnp.concatenate([gain, gain], axis=1)
+    wide_gain = jnp.concatenate([gain] * STEP, axis=1)
 
     def attend(g, pair, head):
         ka, va, kT, vT = head
-        lo = pair * 256
-        cols = slice(lo, lo + 256)
-        full = slice(g * 1024 + lo, g * 1024 + lo + 256)
+        lo = pair * STEP * HD
+        cols = slice(lo, lo + STEP * HD)
+        full = slice(g * 1024 + lo, g * 1024 + lo + STEP * HD)
         scores = jnp.dot(ka, qn[g, :, cols], preferred_element_type=F32)
         m = mask[...]
-        e = jnp.exp2(scores * (SCALE * LOG2E)) * jnp.concatenate([m, m], axis=1)
+        e = jnp.exp2(scores * (SCALE * LOG2E)) * jnp.concatenate([m] * STEP, axis=1)
         total = jnp.sum(e, axis=0, keepdims=True)
         wt = e.astype(BF)
         w_s[:, cols] = wt
@@ -347,9 +348,9 @@
         xhat = xh[:, full]
         r = rq[0:1, full]
         gacc[...] += dy * xhat
-        dxh = dy * gain2
+        dxh = dy * wide_gain
         dx = r * (dxh - xhat * jnp.mean(xhat * dxh, axis=0, keepdims=True))
-        for n in range(2):
+        for n in range(STEP):
             at = slice(g * 1024 + lo + n * HD, g * 1024 + lo + (n + 1) * HD)
             attv[:, at] = attT[:, n * HD:(n + 1) * HD].T.astype(BF)
             dqv[:, at] = dx[:, n * HD:(n + 1) * HD].T.astype(BF)
@@ -508,27 +509,25 @@
     project(3)
 
     todo = {
-        0: [lambda: spread(2), lambda: share(1)],
-        1: [lambda: spread(3)],
-        3: [lambda: c1(0), lambda: share(2)],
-        6: [lambda: c2(0)],
-        7: [lambda: share(3), lambda: c1(1), lambda: weight_share(0)],
-        10: [lambda: c2(1), lambda: weight_share(1)],
-        11: [lambda: c1(2), lambda: c3(0), lambda: weight_share(2)],
-        14: [lambda: c2(2), lambda: weight_share(3)],
-        15: [lambda: c1(3), lambda: c4(0)],
+        0: [lambda: spread(2), lambda: share(1), lambda: spread(3)],
+        1: [lambda: c1(0), lambda: share(2)],
+        3: [lambda: c2(0), lambda: share(3), lambda: c1(1), lambda: weight_share(0)],
+        5: [lambda: c2(1), lambda: c1(2), lambda: weight_share(1), lambda: weight_share(2)],
+        6: [lambda: c3(0), lambda: weight_share(3)],
+        7: [lambda: c1(3), lambda: c2(2)],
     }
     for g in range(KVH):
         head = open_head(g)
-        for pair in range(4):
+        for pair in range(GROUP // STEP):
             attend(g, pair, head)
-            if pair == 3:
+            if pair == GROUP // STEP - 1:
                 close_head(g)
-            for fn in todo.get(g * 4 + pair, ()):
+            for fn in todo.get(g * (GROUP // STEP) + pair, ()):
                 fn()
 
     c3(1)
     c2(3)
+    c4(0)
     c4(1)
     c3(2)
     c3(3, 0)
@@ -542,7 +541,7 @@
     d1(1)
     weight_terms(0)
     scatter(0)
-    a = gacc[:, :HD] + gacc[:, HD:]
+    a = sum(gacc[:, n * HD:(n + 1) * HD] for n in range(STEP))
     gs1[...] = jnp.concatenate(
         [jnp.sum(a.T, axis=0, keepdims=True), kacc[...], jnp.zeros((6, HD), F32)], axis=0
     )
@@ -672,7 +671,7 @@
             vmem((16, 192, HD), BF),
             vmem((16, 192, HD), BF),
             vmem((192, HD), F32),
-            vmem((HD, 256), F32),
+            vmem((HD, STEP * HD), F32),
             vmem((1, HD), F32),
             vmem((8, HD), F32),
             vmem((8, 8, HD), F32),

time: 87.8 us -> 85.7 us (0.976)
  Pallas kernels: 86.8 us -> 84.7 us
    pallas_call x1, Pallas kernels: 84.1 us -> 82 us  [shards(): pl.pallas_call(mega_kernel, out_shape=(sds((TOK, wide), BF), sds((TOK, wi...]
where the time goes in v8:
time: 85.7 us; the launch traced here: 85.6 us
  Pallas kernels  84.7 us (99%)
    pallas_call x1, Pallas kernels, shards(): pl.pallas_call(mega_kernel, out_shape=(sds((TOK, wide), BF), sds((TOK, wi...  82 us
    pallas_call x1, Pallas kernels, shards(): pl.pallas_call(finish_kernel, out_shape=tuple((sds(r.shape, r.dtype) for...  2.74 us

profile of v8, /device:TPU:1, one launch (start us, length us, event | category | flops | bytes accessed | tf_op | source)
XLA Modules:
  0.0 85.6 jit_solution(15570555303946433141)
XLA Ops:
  0.6 82.0 %mega.1 = (bf16[128,4096]{1,0:T(8,128)(2,1)}, bf16[128,4096]{1,0:T(8,128)(2,1)}, bf16[128,2560]{1,0:T(8,128)(2,1)}, bf16[20,1024]{1,0:T(8,128)(2,1)}, f32[1,128]{1,0:T(1,128)}, /*index=5*/f32[1,128]{1,0:T(1,128)}) custom-call(bf16[320,1024]{1,0:T(8,128)(2,1)} %w.1, bf16[128,2560]{1,0:T(8,128)(2,1)} %bitcast.13, bf16[128,4096]{1,0:T(8,128)(2,1)} %bitcast.11, ...), custom_call_target="tpu_custom_call" | custom-call | tf_op jit(solution)/shard_map/mega/pallas_call | solution.py:625
  82.6 2.7 %finish.1 = (bf16[128,4096]{1,0:T(8,128)(2,1)}, bf16[128,4096]{1,0:T(8,128)(2,1)}, bf16[128,2560]{1,0:T(8,128)(2,1)}, bf16[20,1024]{1,0:T(8,128)(2,1)}, f32[1,128]{1,0:T(1,128)}, /*index=5*/f32[1,128]{1,0:T(1,128)}) custom-call(bf16[128,4096]{1,0:T(8,128)(2,1)} %get-tuple-element.18.refs_0_, bf16[128,4096]{1,0:T(8,128)(2,1)} %get-tuple-element.19.refs_1_, ...), custom_call_target="tpu_custom_call" | custom-call | tf_op jit(solution)/shard_map/finish/pallas_call | solution.py:693

commit v9 on v8

--- a/solution.py
+++ b/solution.py
@@ -342,7 +342,7 @@
         dsc = (d_out * inv).astype(BF)
         dos[:, cols] = dsc
         dp = jnp.dot(va, dsc, preferred_element_type=F32)
-        ds = (e * (dp - delta)).astype(BF)
+        ds = (wt.astype(F32) * (dp - delta)).astype(BF)
         ds_s[:, cols] = ds
         dy = jnp.dot(kT, ds, preferred_element_type=F32) * SCALE
         xhat = xh[:, full]

time: 85.7 us -> 86.1 us (level)
  no operation moved by 1% of the time
where the time goes in v9:
time: 86.1 us; the launch traced here: 86 us
  Pallas kernels  85.2 us (99%)
    pallas_call x1, Pallas kernels, shards(): pl.pallas_call(mega_kernel, out_shape=(sds((TOK, wide), BF), sds((TOK, wi...  82.4 us
    pallas_call x1, Pallas kernels, shards(): pl.pallas_call(finish_kernel, out_shape=tuple((sds(r.shape, r.dtype) for...  2.74 us

profile of v9, /device:TPU:1, one launch (start us, length us, event | category | flops | bytes accessed | tf_op | source)
XLA Modules:
  0.0 86.0 jit_solution(8707951413472114110)
XLA Ops:
  0.6 82.4 %mega.1 = (bf16[128,4096]{1,0:T(8,128)(2,1)}, bf16[128,4096]{1,0:T(8,128)(2,1)}, bf16[128,2560]{1,0:T(8,128)(2,1)}, bf16[20,1024]{1,0:T(8,128)(2,1)}, f32[1,128]{1,0:T(1,128)}, /*index=5*/f32[1,128]{1,0:T(1,128)}) custom-call(bf16[320,1024]{1,0:T(8,128)(2,1)} %w.1, bf16[128,2560]{1,0:T(8,128)(2,1)} %bitcast.13, bf16[128,4096]{1,0:T(8,128)(2,1)} %bitcast.11, ...), custom_call_target="tpu_custom_call" | custom-call | tf_op jit(solution)/shard_map/mega/pallas_call | solution.py:625
  83.1 2.7 %finish.1 = (bf16[128,4096]{1,0:T(8,128)(2,1)}, bf16[128,4096]{1,0:T(8,128)(2,1)}, bf16[128,2560]{1,0:T(8,128)(2,1)}, bf16[20,1024]{1,0:T(8,128)(2,1)}, f32[1,128]{1,0:T(1,128)}, /*index=5*/f32[1,128]{1,0:T(1,128)}) custom-call(bf16[128,4096]{1,0:T(8,128)(2,1)} %get-tuple-element.18.refs_0_, bf16[128,4096]{1,0:T(8,128)(2,1)} %get-tuple-element.19.refs_1_, ...), custom_call_target="tpu_custom_call" | custom-call | tf_op jit(solution)/shard_map/finish/pallas_call | solution.py:693
